TPU v7x, 32 devices: a whole 2x2x4 slice. The times are simulated.
32 devices in a mesh: member: 2 (over y), tile: 4 (over z), chan: 4 (over x, core).
Axes of the slice: x: 2, y: 2, z: 4, core: 2. Of those that a mesh axis runs over, the one named last changes fastest.
Arguments:
- latlon_grad: bfloat16 [128, 69, 128], P(('member', 'tile', 'chan')), parts along dimension 0, may hold values from -6 to 6
- remap_weight: bfloat16 [4096, 128, 128], P(('tile', 'chan')), may hold values from -0.5 to 0.5
- src_block: int32 [4096], P(('tile', 'chan')), may hold values from 0 to 3
- owner: int32 [4096], P(('tile', 'chan')), may hold values from 0 to 3, as said below
- target_half: int32 [4096], P(('tile', 'chan')), may hold values from 0 to 13
- live_count: int32 [16], P(('tile', 'chan')), may hold values from 96 to 256
- conv_weight: bfloat16 [9, 69, 256], replicated, may hold values from -0.125 to 0.125
- nbr_block: int32 [112, 4], P(('tile', 'chan')), may hold values from 0 to 111, as said below
- nbr_code: int32 [112, 4], P(('tile', 'chan')), may hold values from 0 to 7, as said below
Outputs:
- hidden_grad: bfloat16 [256, 224, 256], P(None, ('member', 'tile', 'chan')), parts along dimension 1
There are 2 independent parts, one for each index of `member`. A program takes and returns all parts, laid end to end along the dimension named above; an argument that names none is the same for every part. Nothing has to cross between parts.
Inputs may be any that keep to these rules, and one draw needn't show every extreme that they name: `owner`: slots 64 m to 64 m + 63 of one device name one tile index, and different such runs of one device name different tile indices. The neighbour of a block of device index d (over tile+chan, d = block // 7) lies on device index d - 1, d or d + 1, taken cyclically; no block neighbours itself. The tables are symmetric: if nbr_block[g, s] = g' and nbr_code[g, s] = 2 s' + f, then nbr_block[g', s'] = g and nbr_code[g', s'] = 2 s + f. `nbr_code`: see nbr_block.
All inputs are finite; a program needn't handle non-finite values.
Results may differ from a plain program's by a relative error of at most 0.0058.
Values may be sent and summed in bfloat16 or wider, within the bound.
No kernel may reach another device: no remote copies, remote signals or barrier semaphores. Data moves between devices by JAX's collectives and lax.ppermute only.
A program may use at most 64 MiB of HBM per device.

v0:
```python
import jax
import jax.numpy as jnp
import numpy as np
from jax import lax
from jax.experimental import pallas as pl
from jax.experimental.pallas import tpu as pltpu
from jax.sharding import PartitionSpec as P

BF16 = jnp.bfloat16
F32 = jnp.float32
SIDE = 16
CELLS = SIDE * SIDE
LANES = 128
TAPS = 9
VMEM_LIMIT = 48 * 1024 * 1024


def edge_cell(side, position):
    return (
        position,
        SIDE * position,
        SIDE * (SIDE - 1) + position,
        SIDE * position + SIDE - 1,
    )[side]


def lane_order():
    edges = sorted({edge_cell(side, position) for side in range(4) for position in range(SIDE)})
    inner = [cell for cell in range(CELLS) if cell not in set(edges)]
    return edges + inner


def permutation_matrix():
    order = lane_order()
    matrix = np.zeros((CELLS, CELLS), np.float32)
    for lane, cell in enumerate(order):
        matrix[cell, lane] = 1
    return matrix


def shift_matrices():
    order = lane_order()
    matrix = np.zeros((TAPS, CELLS, CELLS), np.float32)
    for tap in range(TAPS):
        down, right = tap // 3 - 1, tap % 3 - 1
        for lane, cell in enumerate(order):
            row, column = cell // SIDE + down, cell % SIDE + right
            if 0 <= row < SIDE and 0 <= column < SIDE:
                matrix[tap, lane, row * SIDE + column] = 1
    return matrix


def edge_matrix():
    lane_of = {cell: lane for lane, cell in enumerate(lane_order())}
    matrix = np.zeros((LANES, 3, 2, 4, SIDE), np.float32)
    for shift in (-1, 0, 1):
        for half in range(2):
            for side in range(4):
                for position in range(SIDE):
                    if 0 <= position - shift < SIDE:
                        lane = lane_of[edge_cell(side, position - shift)]
                        matrix[64 * half + lane, shift + 1, half, side, position] = 1
    return matrix.reshape(LANES, 3 * LANES)


def place_matrix():
    matrix = np.zeros((4, SIDE, CELLS), np.float32)
    for side in range(4):
        for position in range(SIDE):
            matrix[side, position, edge_cell(side, position)] = 1
    return matrix.reshape(4 * SIDE, CELLS)


def rim_taps(side):
    return [((0 + d), 3 * d, 6 + d, 3 * d + 2)[side] for d in range(3)]


def constant(matrix):
    return jnp.asarray(matrix, BF16)


def whole(array):
    rank = array.ndim
    return pl.BlockSpec(array.shape, lambda *_: (0,) * rank)


def remap_runs(
    shifts, latlon_grad, remap_weight, src_block, owner, target_half, live_count, blocks, padded, kept
):
    slots, half = remap_weight.shape[:2]
    channels = latlon_grad.shape[1]
    sources = latlon_grad.shape[0]
    tiles = lax.axis_size("tile")
    run = slots // tiles
    chunk = min(16, run)
    chunks = run // chunk
    halves = 2 * blocks
    count = len(shifts)

    def kernel(*refs):
        live, src_in, tgt_in, own_in, grad_in, weight_in, perm_ref = refs[:7]
        refs = refs[7 + len(kept) :]
        out_refs, refs = refs[: 2 * count], refs[2 * count + len(kept) :]
        src, tgt, own, packed, grad, weight, total, small_sem, weight_sem = refs
        tile = lax.axis_index("tile")
        small = [
            pltpu.make_async_copy(source, target, small_sem.at[index])
            for index, (source, target) in enumerate(
                ((own_in, own), (src_in, src), (tgt_in, tgt), (grad_in, packed))
            )
        ]
        for copy in small:
            copy.start()
        small[0].wait()
        firsts = []
        copies = []
        for place, shift in enumerate(shifts):
            wanted = lax.rem(tile + shift, tiles)
            found = jnp.int32(0)
            for index in range(tiles):
                found = found + jnp.where(own[index * run] == wanted, index, 0)
            firsts.append(found * run)
            for part in range(chunks):
                copies.append(
                    pltpu.make_async_copy(
                        weight_in.at[pl.ds(found * run + part * chunk, chunk)],
                        weight.at[pl.ds(place * run + part * chunk, chunk)],
                        weight_sem.at[place * chunks + part],
                    )
                )
                copies[-1].start()
        total[...] = jnp.zeros_like(total)
        for copy in small[1:]:
            copy.wait()
        wide = packed[...].astype(F32)
        for source in range(sources):
            grad[source] = wide[:, source].astype(BF16)
        for place in range(count):
            for part in range(chunks):
                copies[place * chunks + part].wait()
                for slot in range(part * chunk, (part + 1) * chunk):
                    entry = firsts[place] + slot
                    where = jnp.where(entry < live[0], tgt[entry], halves)
                    total[place, where, :channels, :] += jnp.dot(
                        grad[src[entry]], weight[place * run + slot], preferred_element_type=F32
                    )
            sums = total[place, :halves].reshape(blocks, 2, padded, half)
            moved = jnp.dot(
                sums[:, 0].reshape(blocks * padded, half).astype(BF16),
                perm_ref[:half],
                preferred_element_type=F32,
            ) + jnp.dot(
                sums[:, 1].reshape(blocks * padded, half).astype(BF16),
                perm_ref[half:],
                preferred_element_type=F32,
            )
            out_refs[2 * place][...] = moved[:, :half].astype(BF16)
            out_refs[2 * place + 1][...] = moved[:, half:].astype(BF16)

    perm = constant(permutation_matrix())
    out = jax.ShapeDtypeStruct((blocks * padded, half), BF16)
    there = pl.BlockSpec(memory_space=pltpu.HBM)
    anywhere = pl.BlockSpec(memory_space=pl.ANY)
    here = pl.BlockSpec(memory_space=pltpu.VMEM)
    operands = [
        pltpu.with_memory_space_constraint(operand, pltpu.HBM)
        for operand in (
            src_block,
            target_half,
            owner,
            latlon_grad.transpose(1, 0, 2),
            remap_weight,
        )
    ]
    results = pl.pallas_call(
        kernel,
        in_specs=[pl.BlockSpec(memory_space=pltpu.SMEM)] + [there] * 5 + [here] + [anywhere] * len(kept),
        out_specs=[here] * (2 * count) + [anywhere] * len(kept),
        out_shape=[out] * (2 * count)
        + [jax.ShapeDtypeStruct(value.shape, value.dtype) for value in kept],
        input_output_aliases={7 + index: 2 * count + index for index in range(len(kept))},
        scratch_shapes=[
            pltpu.SMEM((slots,), jnp.int32),
            pltpu.SMEM((slots,), jnp.int32),
            pltpu.SMEM((slots,), jnp.int32),
            pltpu.VMEM((channels, sources, half), BF16),
            pltpu.VMEM((sources, channels, half), BF16),
            pltpu.VMEM((count * run, half, half), BF16),
            pltpu.VMEM((count, halves + 1, padded, half), F32),
            pltpu.SemaphoreType.DMA((4,)),
            pltpu.SemaphoreType.DMA((count * chunks,)),
        ],
        compiler_params=pltpu.CompilerParams(vmem_limit_bytes=VMEM_LIMIT),
        name="remap",
    )(live_count, *operands, perm, *kept)
    return results[0 : 2 * count : 2], results[1 : 2 * count : 2], results[2 * count :]


def sum_edges(parts, blocks, padded):
    pairs = (blocks + 1) // 2

    def kernel(*refs):
        part_refs, sum_ref, edge_ref = refs[:-2], refs[-2], refs[-1]
        total = part_refs[0][...].astype(F32)
        for ref in part_refs[1:]:
            total = total + ref[...].astype(F32)
        sum_ref[...] = total.astype(BF16)
        lane = lax.broadcasted_iota(jnp.int32, (padded, LANES), 1)
        packed = []
        for pair in range(pairs):
            left = total[2 * pair * padded : (2 * pair + 1) * padded]
            if 2 * pair + 1 < blocks:
                right = total[(2 * pair + 1) * padded : (2 * pair + 2) * padded]
                right = pltpu.roll(right, LANES // 2, 1)
            else:
                right = jnp.zeros_like(left)
            packed.append(jnp.where(lane < LANES // 2, left, right))
        edge_ref[...] = jnp.concatenate(packed, axis=0).astype(BF16)

    return pl.pallas_call(
        kernel,
        out_shape=[
            jax.ShapeDtypeStruct((blocks * padded, LANES), BF16),
            jax.ShapeDtypeStruct((pairs * padded, LANES), BF16),
        ],
        compiler_params=pltpu.CompilerParams(vmem_limit_bytes=VMEM_LIMIT),
        name="sum_edges",
    )(*parts)


def prepare(conv_weight, nbr_block, nbr_code, padded, after):
    taps, channels, hidden = conv_weight.shape
    blocks = nbr_block.shape[0]
    pairs = (blocks + 1) // 2
    devices = lax.axis_size(("tile", "chan"))
    columns = 3 * pairs * LANES
    slots = blocks * 4 * SIDE

    def kernel(nbr, code, taps_ref, unread, weight_ref, rim_ref, pick_ref):
        me = lax.axis_index(("tile", "chan"))
        empty = jnp.zeros((padded - channels, hidden), F32)
        rows = []
        for tap in range(taps):
            rows.append(jnp.concatenate([taps_ref[tap].astype(F32), empty], axis=0))
        weight_ref[...] = jnp.concatenate(rows, axis=0).T.astype(BF16)
        for side in range(4):
            chosen = [rows[tap] for tap in rim_taps(side)]
            rim_ref[side * hidden : (side + 1) * hidden] = (
                jnp.concatenate(chosen, axis=0).T.astype(BF16)
            )
        lane = lax.broadcasted_iota(jnp.int32, (1, slots), 1)
        which = lane // SIDE
        position = lane % SIDE
        start = jnp.zeros((1, slots), jnp.int32)
        turned = jnp.zeros((1, slots), jnp.int32)
        for block in range(blocks):
            for side in range(4):
                other = nbr[side, block]
                turn = code[side, block]
                relative = lax.rem(other // blocks - me + 1 + devices, devices)
                column = (relative * 2 * pairs + lax.rem(other, blocks)) * 64 + turn // 2 * SIDE
                start = jnp.where(which == 4 * block + side, column, start)
                turned = jnp.where(which == 4 * block + side, turn % 2, turned)
        source = start + jnp.where(turned == 1, SIDE - 1 - position, position)
        row = lax.broadcasted_iota(jnp.int32, (columns, slots), 0)
        pick_ref[...] = jnp.where(row == source, 1.0, 0.0).astype(BF16)

    smem = pl.BlockSpec(memory_space=pltpu.SMEM)
    vmem = pl.BlockSpec(memory_space=pltpu.VMEM)
    return pl.pallas_call(
        kernel,
        in_specs=[smem, smem, vmem, pl.BlockSpec(memory_space=pl.ANY)],
        out_specs=[vmem] * 3,
        out_shape=[
            jax.ShapeDtypeStruct((hidden, taps * padded), BF16),
            jax.ShapeDtypeStruct((4 * hidden, 3 * padded), BF16),
            jax.ShapeDtypeStruct((columns, slots), BF16),
        ],
        compiler_params=pltpu.CompilerParams(vmem_limit_bytes=VMEM_LIMIT),
        name="prepare",
    )(nbr_block.T, nbr_code.T, conv_weight, after)


def incoming_rims(edges, rim_weight, pick, blocks, padded):
    pairs = (blocks + 1) // 2
    hidden = rim_weight.shape[0] // 4
    groups = 3 * pairs
    slots = pick.shape[1]

    def kernel(before_ref, own_ref, after_ref, weight_ref, pick_ref, edge_ref, out_ref):
        sides = lax.broadcasted_iota(jnp.int32, (hidden, 2 * LANES), 1) // SIDE % 4
        stacks = []
        for ref in (before_ref, own_ref, after_ref):
            shifted = jnp.dot(ref[...], edge_ref[...], preferred_element_type=F32)
            for pair in range(pairs):
                rows = shifted[pair * padded : (pair + 1) * padded]
                stacks.append(
                    jnp.concatenate([rows[:, LANES * d : LANES * (d + 1)] for d in range(3)], axis=0)
                )
        total = jnp.zeros((hidden, slots), F32)
        for group in range(0, groups, 2):
            stack = jnp.concatenate(stacks[group : group + 2], axis=1).astype(BF16)
            width = stack.shape[1]
            every = jnp.dot(weight_ref[...], stack, preferred_element_type=F32)
            rims = every[:hidden]
            for side in range(1, 4):
                rims = jnp.where(
                    sides[:, :width] == side, every[side * hidden : (side + 1) * hidden], rims
                )
            total = total + jnp.dot(
                rims.astype(BF16),
                pick_ref[group * LANES : group * LANES + width],
                preferred_element_type=F32,
            )
        out_ref[...] = total.astype(BF16)

    return pl.pallas_call(
        kernel,
        out_shape=jax.ShapeDtypeStruct((hidden, slots), BF16),
        compiler_params=pltpu.CompilerParams(vmem_limit_bytes=VMEM_LIMIT),
        name="rims",
    )(*edges, rim_weight, pick, constant(edge_matrix()))


def convolve(first, second_parts, weight, incoming, blocks, padded):
    hidden = weight.shape[0]
    parts = len(second_parts)

    def kernel(*refs):
        first_ref, part_refs = refs[0], refs[1 : 1 + parts]
        weight_ref, incoming_ref, shift_ref, place_ref = refs[1 + parts : 5 + parts]
        out_ref, stack = refs[5 + parts :]
        total = part_refs[0][...].astype(F32)
        for ref in part_refs[1:]:
            total = total + ref[...].astype(F32)
        second = total.astype(BF16)
        for tap in range(TAPS):
            moved = jnp.dot(
                first_ref[...], shift_ref[tap, :LANES], preferred_element_type=F32
            ) + jnp.dot(second, shift_ref[tap, LANES:], preferred_element_type=F32)
            stack[:, padded * tap : padded * (tap + 1), :] = moved.reshape(blocks, padded, CELLS)
        for block in range(blocks):
            grad = jnp.dot(
                weight_ref[...], stack[block].astype(BF16), preferred_element_type=F32
            ) + jnp.dot(
                incoming_ref[:, 64 * block : 64 * (block + 1)],
                place_ref[...],
                preferred_element_type=F32,
            )
            out_ref[block] = grad.astype(BF16)

    return pl.pallas_call(
        kernel,
        out_shape=jax.ShapeDtypeStruct((blocks, hidden, CELLS), BF16),
        scratch_shapes=[pltpu.VMEM((blocks, TAPS * padded, CELLS), F32)],
        compiler_params=pltpu.CompilerParams(vmem_limit_bytes=VMEM_LIMIT),
        name="convolve",
    )(
        first,
        *second_parts,
        weight,
        incoming,
        constant(shift_matrices()),
        constant(place_matrix()),
    )


def from_behind(value, axis, steps):
    count = lax.axis_size(axis)
    pairs = [(source, (source + steps) % count) for source in range(count)]
    return lax.ppermute(value, axis, pairs)


def summed_here(
    latlon_grad, remap_weight, src_block, owner, target_half, live_count, blocks, padded
):
    tiles = lax.axis_size("tile")
    operands = (
        latlon_grad, remap_weight, src_block, owner, target_half, live_count, blocks, padded
    )
    lead = tiles // 2
    shifts = [shift for shift in range(1, tiles) if shift != lead] + [0]
    (first,), (second,), _ = remap_runs([lead], *operands, ())
    first_parts = [from_behind(first, "tile", lead)]
    firsts, seconds, (second,) = remap_runs(shifts, *operands, (second,))
    first_parts += [from_behind(part, "tile", shift) for part, shift in zip(firsts, shifts) if shift]
    second_parts = [from_behind(second, "tile", lead)]
    second_parts += [from_behind(part, "tile", shift) for part, shift in zip(seconds, shifts) if shift]
    return first_parts + [firsts[-1]], second_parts + [seconds[-1]]


def summed_there(
    latlon_grad, remap_weight, src_block, owner, target_half, live_count, blocks, padded
):
    slots, half = remap_weight.shape[:2]
    channels = latlon_grad.shape[1]
    tiles = lax.axis_size("tile")
    run = slots // tiles
    live = jnp.arange(slots, dtype=jnp.int32) < live_count[0]
    runs = jnp.argsort(owner.reshape(tiles, run)[:, 0])
    picked = jnp.take(latlon_grad, src_block, axis=0)
    product = jnp.einsum("eoa,eab->eob", picked, remap_weight, preferred_element_type=F32)
    product = jnp.where(live[:, None, None], product, 0).astype(BF16)
    outgoing = jnp.take(product.reshape(tiles, run, channels, half), runs, axis=0)
    ids = jnp.take(target_half.reshape(tiles, run), runs, axis=0)
    arrived = lax.all_to_all(outgoing, "tile", split_axis=0, concat_axis=0, tiled=True)
    ids = lax.all_to_all(ids, "tile", split_axis=0, concat_axis=0, tiled=True).reshape(slots)
    selector = (jnp.arange(2 * blocks, dtype=jnp.int32)[:, None] == ids[None, :]).astype(BF16)
    sums = jnp.einsum(
        "hs,soa->hoa",
        selector,
        arrived.reshape(slots, channels, half),
        preferred_element_type=F32,
    ).astype(BF16)
    cells = sums.reshape(blocks, 2, channels, half).transpose(0, 2, 1, 3)
    cells = cells.reshape(blocks, channels, 2 * half)[:, :, np.array(lane_order())]
    cells = jnp.pad(cells, ((0, 0), (0, padded - channels), (0, 0)))
    cells = cells.reshape(blocks * padded, 2 * half)
    return [cells[:, :half]], [cells[:, half:]]


def per_device(
    latlon_grad,
    remap_weight,
    src_block,
    owner,
    target_half,
    live_count,
    conv_weight,
    nbr_block,
    nbr_code,
):
    channels = latlon_grad.shape[1]
    hidden = conv_weight.shape[2]
    blocks = nbr_block.shape[0]
    padded = 8 * ((channels + 7) // 8)
    run = remap_weight.shape[0] // lax.axis_size("tile")
    gather = summed_here if run >= 2 * blocks else summed_there
    first_parts, second_parts = gather(
        latlon_grad, remap_weight, src_block, owner, target_half, live_count, blocks, padded
    )
    weight, rim_weight, pick = prepare(conv_weight, nbr_block, nbr_code, padded, first_parts[-1])
    first, edges = sum_edges(first_parts, blocks, padded)
    before = from_behind(edges, ("tile", "chan"), 1)
    after = from_behind(edges, ("tile", "chan"), -1)
    incoming = incoming_rims((before, edges, after), rim_weight, pick, blocks, padded)
    grads = convolve(first, second_parts, weight, incoming, blocks, padded)
    return grads.transpose(1, 0, 2)


def solution(mesh):
    in_specs = (
        P(("member", "tile", "chan"), None, None),
        P(("tile", "chan"), None, None),
        P(("tile", "chan")),
        P(("tile", "chan")),
        P(("tile", "chan")),
        P(("tile", "chan")),
        P(),
        P(("tile", "chan"), None),
        P(("tile", "chan"), None),
    )
    out_specs = P(None, ("member", "tile", "chan"), None)
    return jax.shard_map(
        per_device, mesh=mesh, in_specs=in_specs, out_specs=out_specs, check_vma=False
    )
```

profile of v0, /device:TPU:0, one launch (start us, length us, event | category | flops | bytes accessed | tf_op | source)
XLA Modules:
  0.0 41.2 jit_solution(6047434866974592998)
XLA Ops:
  0.7 0.0 copy-start.1
  0.7 0.9 %copy-done.1 = bf16[256,256]{1,0:T(8,128)(2,1)S(1)} copy-done((bf16[256,256]{1,0:T(8,128)(2,1)S(1)}, bf16[256,256]{1,0:T(8,128)(2,1)}, u32[]{:S(2)}) %copy-start.1) | copy-done | bytes 131096
  1.6 3.4 %remap.2 = (bf16[504,128]{1,0:T(8,128)(2,1)S(1)}, bf16[504,128]{1,0:T(8,128)(2,1)S(1)}) custom-call(s32[1]{0:T(128)S(6)} %copy.17.refs_0_, s32[256]{0:T(256)} %refs_1_.3, s32[256]{0:T(256)} %refs_2_.3, s32[256]{0:T(256)} %refs_3_.3, bf16[69,4,128]{2,1,0:T(4,128)(2,1)} %bitcast.6, bf16[256,128,128]{2,1,0:T(8,128)(2,1)} %refs_5_.3, bf16[256,256]{1,0:T(8,128)(2,1)S(1)} %copy-done.1), custom_call_target="tpu_custom_call" | custom-call | tf_op jit(solution)/shard_map/remap/pallas_call | solution.py:175
  5.0 4.1 %collective-permute-start = (bf16[504,128]{1,0:T(8,128)(2,1)S(1)}, bf16[504,128]{1,0:T(8,128)(2,1)S(1)}, u32[]{:S(2)}, u32[]{:S(2)}) collective-permute-start(bf16[504,128]{1,0:T(8,128)(2,1)S(1)} %get-tuple-element.19), channel_id=1, source_target_pairs={{0,8},{4,12},{8,0},{12,4},{1,9},{5,13},{9,1},{13,5},{2,10},{6,14},... | collective-permute-start | bytes 387080 | tf_op jit(solution)/shard_map/ppermute | solution.py:371
  9.1 7.3 %remap.3 = (bf16[504,128]{1,0:T(8,128)(2,1)S(1)}, bf16[504,128]{1,0:T(8,128)(2,1)S(1)}, bf16[504,128]{1,0:T(8,128)(2,1)S(1)}, bf16[504,128]{1,0:T(8,128)(2,1)S(1...) custom-call(s32[1]{0:T(128)S(6)} %copy.17.refs_0_, ...), custom_call_target="tpu_custom_call", output_to_operand_aliasing={{6}: (7, {})} | custom-call | tf_op jit(solution)/shard_map/remap/pallas_call | solution.py:175
  16.5 1.6 %collective-permute-start.1 = (bf16[504,128]{1,0:T(8,128)(2,1)S(1)}, bf16[504,128]{1,0:T(8,128)(2,1)S(1)}, u32[]{:S(2)}, u32[]{:S(2)}) collective-permute-start(bf16[504,128]{1,0:T(8,128)(2,1)S(1)} %get-tuple-element.21), channel_id=1, source_target_pairs={{0,4},{4,8},{8,12},{12,0},{1,5},{5,9},{9,13},{13,1},{2,6},{6,10},{... | collective-permute-start | bytes 387080 | tf_op jit(solution)/shard_map/ppermute | solution.py:371
  18.1 2.2 %collective-permute-start.2 = (bf16[504,128]{1,0:T(8,128)(2,1)S(1)}, bf16[504,128]{1,0:T(8,128)(2,1)S(1)}, u32[]{:S(2)}, u32[]{:S(2)}) collective-permute-start(bf16[504,128]{1,0:T(8,128)(2,1)S(1)} %get-tuple-element.22), channel_id=1, source_target_pairs={{0,12},{4,0},{8,4},{12,8},{1,13},{5,1},{9,5},{13,9},{2,14},{6,2},{... | collective-permute-start | bytes 387080 | tf_op jit(solution)/shard_map/ppermute | solution.py:371
  20.4 0.6 %collective-permute-start.4 = (bf16[504,128]{1,0:T(8,128)(2,1)S(1)}, bf16[504,128]{1,0:T(8,128)(2,1)S(1)}, u32[]{:S(2)}, u32[]{:S(2)}) collective-permute-start(bf16[504,128]{1,0:T(8,128)(2,1)S(1)} %get-tuple-element.26), channel_id=1, source_target_pairs={{0,4},{4,8},{8,12},{12,0},{1,5},{5,9},{9,13},{13,1},{2,6},{6,10},{... | collective-permute-start | bytes 387080 | tf_op jit(solution)/shard_map/ppermute | solution.py:371
  20.9 0.0 collective-permute-done.refs_0_
  20.9 3.3 %collective-permute-start.5 = (bf16[504,128]{1,0:T(8,128)(2,1)S(1)}, bf16[504,128]{1,0:T(8,128)(2,1)S(1)}, u32[]{:S(2)}, u32[]{:S(2)}) collective-permute-start(bf16[504,128]{1,0:T(8,128)(2,1)S(1)} %get-tuple-element.27), channel_id=1, source_target_pairs={{0,12},{4,0},{8,4},{12,8},{1,13},{5,1},{9,5},{13,9},{2,14},{6,2},{... | collective-permute-start | bytes 387080 | tf_op jit(solution)/shard_map/ppermute | solution.py:371
  24.2 0.5 %collective-permute-done.1.refs_1_ = bf16[504,128]{1,0:T(8,128)(2,1)S(1)} collective-permute-done((bf16[504,128]{1,0:T(8,128)(2,1)S(1)}, bf16[504,128]{1,0:T(8,128)(2,1)S(1)}, u32[]{:S(2)}, u32[]{:S(2)}) %collective-permute-start.1) | collective-permute-done | bytes 129056 | tf_op jit(solution)/shard_map/ppermute | solution.py:371
  24.7 2.1 %collective-permute-done.2.refs_2_ = bf16[504,128]{1,0:T(8,128)(2,1)S(1)} collective-permute-done((bf16[504,128]{1,0:T(8,128)(2,1)S(1)}, bf16[504,128]{1,0:T(8,128)(2,1)S(1)}, u32[]{:S(2)}, u32[]{:S(2)}) %collective-permute-start.2) | collective-permute-done | bytes 129056 | tf_op jit(solution)/shard_map/ppermute | solution.py:371
  26.8 0.1 sum_edges.1
  26.9 0.6 %collective-permute-start.7 = (bf16[288,128]{1,0:T(8,128)(2,1)S(1)}, bf16[288,128]{1,0:T(8,128)(2,1)S(1)}, u32[]{:S(2)}, u32[]{:S(2)}) collective-permute-start(bf16[288,128]{1,0:T(8,128)(2,1)S(1)} %get-tuple-element.30.own_ref), channel_id=1, source_target_pairs={{0,15},{1,0},{2,1},{3,2},{4,3},{5,4},{6,5},{7,6},{8,7},{9,8},{10,9... | collective-permute-start | bytes 221192 | tf_op jit(solution)/shard_map/ppermute | solution.py:371
  27.5 0.0 collective-permute-start.6
  27.5 0.0 copy-start
  27.5 0.0 copy-start.4
  27.5 1.9 %prepare.1 = (bf16[256,648]{1,0:T(8,128)(2,1)S(1)}, bf16[1024,216]{1,0:T(8,128)(2,1)S(1)}, bf16[1536,448]{1,0:T(8,128)(2,1)S(1)}) custom-call(s32[4,7]{1,0:T(4,128)S(1)} %bitcast.4, s32[4,7]{1,0:T(4,128)S(1)} %bitcast.5, bf16[9,69,256]{2,1,0:T(8,128)(2,1)S(1)} %copy-done.2, bf16[504,128]{1,0:T(8,128)(2,1)S(1)} %get-tuple-element.23.refs_3_.unread), custom_call_target="tpu_custom_call" | custom-call | tf_op jit(solution)/shard_map/prepare/pallas_call | solution.py:270
  29.4 3.1 %collective-permute-done.7.after_ref = bf16[288,128]{1,0:T(8,128)(2,1)S(1)} collective-permute-done((bf16[288,128]{1,0:T(8,128)(2,1)S(1)}, bf16[288,128]{1,0:T(8,128)(2,1)S(1)}, u32[]{:S(2)}, u32[]{:S(2)}) %collective-permute-start.7) | collective-permute-done | bytes 73760 | tf_op jit(solution)/shard_map/ppermute | solution.py:371
  32.5 2.9 %collective-permute-done.6.before_ref = bf16[288,128]{1,0:T(8,128)(2,1)S(1)} collective-permute-done((bf16[288,128]{1,0:T(8,128)(2,1)S(1)}, bf16[288,128]{1,0:T(8,128)(2,1)S(1)}, u32[]{:S(2)}, u32[]{:S(2)}) %collective-permute-start.6) | collective-permute-done | bytes 73760 | tf_op jit(solution)/shard_map/ppermute | solution.py:371
  35.3 2.5 %rims.1.refs_6_ = bf16[256,448]{1,0:T(8,128)(2,1)S(1)} custom-call(bf16[288,128]{1,0:T(8,128)(2,1)S(1)} %collective-permute-done.6.before_ref, bf16[288,128]{1,0:T(8,128)(2,1)S(1)} %get-tuple-element.30.own_ref, bf16[288,128]{1,0:T(8,128)(2,1)S(1)} %collective-permute-done.7.after_ref, bf16[1024,216]{1,0:T(8,128)(2,1)S(1)} %get-tuple-element.31.weight_ref, ...), custom_call_target="tpu_custom_call" | custom-call | tf_op jit(solution)/shard_map/rims/pallas_call | solution.py:317
  37.8 0.0 collective-permute-done.3.refs_1_
  37.9 0.0 collective-permute-done.4.refs_2_
  37.9 3.3 %convolve.1 = bf16[7,256,256]{2,1,0:T(8,128)(2,1)} custom-call(bf16[504,128]{1,0:T(8,128)(2,1)S(1)} %get-tuple-element.24.refs_0_, bf16[504,128]{1,0:T(8,128)(2,1)S(1)} %collective-permute-done.3.refs_1_, bf16[504,128]{1,0:T(8,128)(2,1)S(1)} %collective-permute-done.4.refs_2_, bf16[504,128]{1,0:T(8,128)(2,1)S(1)} %collective-permute-done.5.refs_3_, ...), custom_call_target="tpu_custom_call" | custom-call | tf_op jit(solution)/shard_map/convolve/pallas_call | solution.py:352
  (12 shorter events, 0.0 us)
Async XLA Ops:
  0.7 0.9 %copy-start.1 = (bf16[256,256]{1,0:T(8,128)(2,1)S(1)}, bf16[256,256]{1,0:T(8,128)(2,1)}, u32[]{:S(2)}) copy-start(bf16[256,256]{1,0:T(8,128)(2,1)} %constant.8.clone.refs_6_) | copy-start | bytes 393220
  5.0 15.9 %collective-permute-start = (bf16[504,128]{1,0:T(8,128)(2,1)S(1)}, bf16[504,128]{1,0:T(8,128)(2,1)S(1)}, u32[]{:S(2)}, u32[]{:S(2)}) collective-permute-start(bf16[504,128]{1,0:T(8,128)(2,1)S(1)} %get-tuple-element.19), channel_id=1, source_target_pairs={{0,8},{4,12},{8,0},{12,4},{1,9},{5,13},{9,1},{13,5},{2,10},{6,14},... | collective-permute-start | bytes 387080 | tf_op jit(solution)/shard_map/ppermute | solution.py:371
  9.1 18.3 %copy-start.2 = (bf16[9,69,256]{2,1,0:T(8,128)(2,1)S(1)}, bf16[9,69,256]{2,1,0:T(8,128)(2,1)}, u32[]{:S(2)}) copy-start(bf16[9,69,256]{2,1,0:T(8,128)(2,1)} %taps_ref.1) | copy-start | bytes 953860
  9.1 18.3 %copy-start.5 = (s32[7,4]{0,1:T(4,128)S(1)}, s32[7,4]{0,1:T(4,128)}, u32[]{:S(2)}) copy-start(s32[7,4]{0,1:T(4,128)} %param.21) | copy-start | bytes 340
  9.1 18.4 %copy-start.6 = (s32[7,4]{0,1:T(4,128)S(1)}, s32[7,4]{0,1:T(4,128)}, u32[]{:S(2)}) copy-start(s32[7,4]{0,1:T(4,128)} %param.22) | copy-start | bytes 340
  9.1 26.2 %copy-start.3 = (bf16[128,384]{1,0:T(8,128)(2,1)S(1)}, bf16[128,384]{1,0:T(8,128)(2,1)}, u32[]{:S(2)}) copy-start(bf16[128,384]{1,0:T(8,128)(2,1)} %constant.9.clone.edge_ref) | copy-start | bytes 294916
  16.5 8.2 %collective-permute-start.1 = (bf16[504,128]{1,0:T(8,128)(2,1)S(1)}, bf16[504,128]{1,0:T(8,128)(2,1)S(1)}, u32[]{:S(2)}, u32[]{:S(2)}) collective-permute-start(bf16[504,128]{1,0:T(8,128)(2,1)S(1)} %get-tuple-element.21), channel_id=1, source_target_pairs={{0,4},{4,8},{8,12},{12,0},{1,5},{5,9},{9,13},{13,1},{2,6},{6,10},{... | collective-permute-start | bytes 387080 | tf_op jit(solution)/shard_map/ppermute | solution.py:371
  18.1 8.7 %collective-permute-start.2 = (bf16[504,128]{1,0:T(8,128)(2,1)S(1)}, bf16[504,128]{1,0:T(8,128)(2,1)S(1)}, u32[]{:S(2)}, u32[]{:S(2)}) collective-permute-start(bf16[504,128]{1,0:T(8,128)(2,1)S(1)} %get-tuple-element.22), channel_id=1, source_target_pairs={{0,12},{4,0},{8,4},{12,8},{1,13},{5,1},{9,5},{13,9},{2,14},{6,2},{... | collective-permute-start | bytes 387080 | tf_op jit(solution)/shard_map/ppermute | solution.py:371
  20.3 17.5 %collective-permute-start.3 = (bf16[504,128]{1,0:T(8,128)(2,1)S(1)}, bf16[504,128]{1,0:T(8,128)(2,1)S(1)}, u32[]{:S(2)}, u32[]{:S(2)}) collective-permute-start(bf16[504,128]{1,0:T(8,128)(2,1)S(1)} %get-tuple-element.25), channel_id=1, source_target_pairs={{0,8},{4,12},{8,0},{12,4},{1,9},{5,13},{9,1},{13,5},{2,10},{6,14},... | collective-permute-start | bytes 387080 | tf_op jit(solution)/shard_map/ppermute | solution.py:371
  20.4 17.5 %collective-permute-start.4 = (bf16[504,128]{1,0:T(8,128)(2,1)S(1)}, bf16[504,128]{1,0:T(8,128)(2,1)S(1)}, u32[]{:S(2)}, u32[]{:S(2)}) collective-permute-start(bf16[504,128]{1,0:T(8,128)(2,1)S(1)} %get-tuple-element.26), channel_id=1, source_target_pairs={{0,4},{4,8},{8,12},{12,0},{1,5},{5,9},{9,13},{13,1},{2,6},{6,10},{... | collective-permute-start | bytes 387080 | tf_op jit(solution)/shard_map/ppermute | solution.py:371
  20.9 17.0 %collective-permute-start.5 = (bf16[504,128]{1,0:T(8,128)(2,1)S(1)}, bf16[504,128]{1,0:T(8,128)(2,1)S(1)}, u32[]{:S(2)}, u32[]{:S(2)}) collective-permute-start(bf16[504,128]{1,0:T(8,128)(2,1)S(1)} %get-tuple-element.27), channel_id=1, source_target_pairs={{0,12},{4,0},{8,4},{12,8},{1,13},{5,1},{9,5},{13,9},{2,14},{6,2},{... | collective-permute-start | bytes 387080 | tf_op jit(solution)/shard_map/ppermute | solution.py:371
  26.9 5.6 %collective-permute-start.7 = (bf16[288,128]{1,0:T(8,128)(2,1)S(1)}, bf16[288,128]{1,0:T(8,128)(2,1)S(1)}, u32[]{:S(2)}, u32[]{:S(2)}) collective-permute-start(bf16[288,128]{1,0:T(8,128)(2,1)S(1)} %get-tuple-element.30.own_ref), channel_id=1, source_target_pairs={{0,15},{1,0},{2,1},{3,2},{4,3},{5,4},{6,5},{7,6},{8,7},{9,8},{10,9... | collective-permute-start | bytes 221192 | tf_op jit(solution)/shard_map/ppermute | solution.py:371
  27.5 7.9 %collective-permute-start.6 = (bf16[288,128]{1,0:T(8,128)(2,1)S(1)}, bf16[288,128]{1,0:T(8,128)(2,1)S(1)}, u32[]{:S(2)}, u32[]{:S(2)}) collective-permute-start(bf16[288,128]{1,0:T(8,128)(2,1)S(1)} %get-tuple-element.30.own_ref), channel_id=1, source_target_pairs={{0,1},{1,2},{2,3},{3,4},{4,5},{5,6},{6,7},{7,8},{8,9},{9,10},{10,1... | collective-permute-start | bytes 221192 | tf_op jit(solution)/shard_map/ppermute | solution.py:371
  27.5 10.4 %copy-start = (bf16[9,256,256]{2,1,0:T(8,128)(2,1)S(1)}, bf16[9,256,256]{2,1,0:T(8,128)(2,1)}, u32[]{:S(2)}) copy-start(bf16[9,256,256]{2,1,0:T(8,128)(2,1)} %constant.10.clone.refs_7_) | copy-start | bytes 3538948
  27.5 10.4 %copy-start.4 = (bf16[64,256]{1,0:T(8,128)(2,1)S(1)}, bf16[64,256]{1,0:T(8,128)(2,1)}, u32[]{:S(2)}) copy-start(bf16[64,256]{1,0:T(8,128)(2,1)} %constant.11.clone.refs_8_) | copy-start | bytes 98308
where the time goes:
time: 41.5 us; the launch traced here: 41.2 us
  Pallas kernels  18.6 us (45%)
  starting transfers between devices  12.4 us (30%)
  waiting for transfers between devices  8.56 us (21%)
  local copies, waits for them, and re-layouts  0.93 us (2%)
  between operations  0.77 us (2%)
    ppermute x8, starting transfers between devices, from_behind(): return lax.ppermute(value, axis, pairs)  12.4 us
    pallas_call x2, Pallas kernels, remap_runs(): pl.pallas_call(kernel, in_specs=[pl.BlockSpec(memory_space=pltpu.SMEM)] +...  10.7 us
    ppermute x8, waiting for transfers between devices, from_behind(): return lax.ppermute(value, axis, pairs)  8.56 us
    pallas_call x1, Pallas kernels, convolve(): pl.pallas_call(kernel, out_shape=jax.ShapeDtypeStruct((blocks, hidden, CE...  3.34 us
    pallas_call x1, Pallas kernels, incoming_rims(): pl.pallas_call(kernel, out_shape=jax.ShapeDtypeStruct((hidden, slots), BF...  2.5 us
    pallas_call x1, Pallas kernels, prepare(): pl.pallas_call(kernel, in_specs=[smem, smem, vmem, pl.BlockSpec(memory_sp...  1.89 us
    unnamed x14, local copies, waits for them, and re-layouts  0.93 us
  transfers between devices with their start and end apart: 8, of which 4 were waited for; matrix products, arithmetic and copies ran while one was open for 0% of the time, Pallas kernels for 29%

commit v1 on v0

v1 whole, which is shorter than its diff:
```python
import functools

import jax
import jax.numpy as jnp
import numpy as np
from jax import lax
from jax.experimental import pallas as pl
from jax.experimental.pallas import tpu as pltpu
from jax.sharding import PartitionSpec as P

BF16 = jnp.bfloat16
F32 = jnp.float32
SIDE = 16
CELLS = SIDE * SIDE
LANES = 128
TAPS = 9
VMEM_LIMIT = 48 * 1024 * 1024
PIECES = 3


def edge_cell(side, position):
    return (
        position,
        SIDE * position,
        SIDE * (SIDE - 1) + position,
        SIDE * position + SIDE - 1,
    )[side]


def lane_order():
    edges = sorted({edge_cell(side, position) for side in range(4) for position in range(SIDE)})
    inner = [cell for cell in range(CELLS) if cell not in set(edges)]
    return edges + inner


def permutation_matrix():
    order = lane_order()
    matrix = np.zeros((CELLS, CELLS), np.float32)
    for lane, cell in enumerate(order):
        matrix[cell, lane] = 1
    return matrix


def shift_matrices():
    order = lane_order()
    matrix = np.zeros((TAPS, CELLS, CELLS), np.float32)
    for tap in range(TAPS):
        down, right = tap // 3 - 1, tap % 3 - 1
        for lane, cell in enumerate(order):
            row, column = cell // SIDE + down, cell % SIDE + right
            if 0 <= row < SIDE and 0 <= column < SIDE:
                matrix[tap, lane, row * SIDE + column] = 1
    return matrix


def edge_matrix(pairs):
    lane_of = {cell: lane for lane, cell in enumerate(lane_order())}
    matrix = np.zeros((pairs, 2, 64, 3, 4, pairs, 2, SIDE), np.float32)
    for shift in (-1, 0, 1):
        for side in range(4):
            for position in range(SIDE):
                if 0 <= position - shift < SIDE:
                    lane = lane_of[edge_cell(side, position - shift)]
                    for pair in range(pairs):
                        for half in range(2):
                            matrix[pair, half, lane, shift + 1, side, pair, half, position] = 1
    return matrix.reshape(pairs * LANES, 12 * 2 * SIDE * pairs)


def place_matrix():
    matrix = np.zeros((4, SIDE, CELLS), np.float32)
    for side in range(4):
        for position in range(SIDE):
            matrix[side, position, edge_cell(side, position)] = 1
    return matrix.reshape(4 * SIDE, CELLS)


def rim_taps(side):
    return [((0 + d), 3 * d, 6 + d, 3 * d + 2)[side] for d in range(3)]


def pack_matrices():
    even = permutation_matrix()
    odd = np.concatenate([even[:, 64:128], even[:, :64], even[:, 128:]], axis=1)
    return np.stack([even, odd])


def constant(matrix):
    return jnp.asarray(matrix, BF16)


def whole(array):
    rank = array.ndim
    return pl.BlockSpec(array.shape, lambda *_: (0,) * rank)


def piece_rows(blocks, padded):
    tiles = 2 * blocks
    cuts = [-(-tiles * index // PIECES) for index in range(PIECES + 1)]
    cuts[1] = max(cuts[1], (blocks + 1) // 2)
    return [(first * padded, last * padded) for first, last in zip(cuts[:-1], cuts[1:])]


def remap_runs(
    flips,
    kind,
    latlon_grad,
    remap_weight,
    src_block,
    owner,
    target_half,
    live_count,
    blocks,
    padded,
    after=(),
):
    slots, half = remap_weight.shape[:2]
    channels = latlon_grad.shape[1]
    sources = latlon_grad.shape[0]
    tiles = lax.axis_size("tile")
    run = slots // tiles
    count = len(flips)
    halves = 2 * blocks
    odds = blocks // 2
    pieces = piece_rows(blocks, padded)
    cuts = [0, run // 2] + [run * (index + 1) for index in range(count)]

    def kernel(*refs):
        live, src_in, tgt_in, own_in, grad_in, weight_in, pack_in = refs[:7]
        refs = refs[7 + len(after) :]
        out_refs, refs = refs[: len(pieces)], refs[len(pieces) :]
        src, tgt, own, packed, grad, weight, pack, total, small_sem, weight_sem = refs
        tile = lax.axis_index("tile")
        small = [
            pltpu.make_async_copy(source, target, small_sem.at[index])
            for index, (source, target) in enumerate(
                (
                    (own_in, own),
                    (src_in, src),
                    (tgt_in, tgt),
                    (grad_in, packed),
                    (pack_in, pack),
                )
            )
        ]
        for copy in small[:4]:
            copy.start()
        small[0].wait()
        firsts = []
        for flip in flips:
            wanted = lax.bitwise_xor(tile, flip)
            found = jnp.int32(0)
            for index in range(tiles):
                found = found + jnp.where(own[index * run] == wanted, index, 0)
            firsts.append(found * run)
        large = []
        for part, (start, stop) in enumerate(zip(cuts[:-1], cuts[1:])):
            first = firsts[start // run] + start % run
            large.append(
                pltpu.make_async_copy(
                    weight_in.at[pl.ds(first, stop - start)],
                    weight.at[pl.ds(start, stop - start)],
                    weight_sem.at[part],
                )
            )
            large[-1].start()
        small[4].start()
        total[...] = jnp.zeros_like(total)
        for copy in small[1:4]:
            copy.wait()
        wide = packed[...].astype(F32)
        for source in range(sources):
            grad[source] = wide[:, source].astype(BF16)
        lane = lax.broadcasted_iota(jnp.int32, (odds * padded, half), 1)
        for part, (start, stop) in enumerate(zip(cuts[:-1], cuts[1:])):
            large[part].wait()
            index = start // run
            for slot in range(start, stop):
                entry = firsts[index] + slot % run
                where = jnp.where(entry < live[0], tgt[entry], halves)
                total[index, where, :channels, :] += jnp.dot(
                    grad[src[entry]], weight[slot], preferred_element_type=F32
                )
            if stop % run:
                continue
            if index == 0:
                small[4].wait()
            moved = []
            for parity in range(2):
                joined = jnp.concatenate(
                    [
                        jnp.concatenate(
                            [total[index, 2 * block], total[index, 2 * block + 1]], axis=1
                        )
                        for block in range(parity, blocks, 2)
                    ],
                    axis=0,
                )
                moved.append(
                    jnp.dot(joined.astype(BF16), pack[parity], preferred_element_type=F32)
                )
            both = odds * padded
            edges = jnp.where(lane < 64, moved[0][:both, :half], moved[1][:, :half])
            middle = jnp.where(lane < 64, moved[1][:, :half], moved[0][:both, :half])
            rows = jnp.concatenate(
                [
                    edges,
                    moved[0][both:, :half],
                    middle,
                    moved[0][:, half:],
                    moved[1][:, half:],
                ],
                axis=0,
            )
            for ref, (first, last) in zip(out_refs, pieces):
                size = last - first
                ref[size * index : size * (index + 1)] = rows[first:last].astype(kind)

    operands = [
        pltpu.with_memory_space_constraint(operand, pltpu.HBM)
        for operand in (
            src_block,
            target_half,
            owner,
            latlon_grad.transpose(1, 0, 2),
            remap_weight,
            constant(pack_matrices()),
        )
    ]
    return pl.pallas_call(
        kernel,
        in_specs=[pl.BlockSpec(memory_space=pltpu.SMEM)]
        + [pl.BlockSpec(memory_space=pltpu.HBM)] * 6
        + [pl.BlockSpec(memory_space=pl.ANY)] * len(after),
        out_specs=[pl.BlockSpec(memory_space=pltpu.VMEM)] * len(pieces),
        out_shape=[
            jax.ShapeDtypeStruct((count * (last - first), half), kind) for first, last in pieces
        ],
        scratch_shapes=[
            pltpu.SMEM((slots,), jnp.int32),
            pltpu.SMEM((slots,), jnp.int32),
            pltpu.SMEM((slots,), jnp.int32),
            pltpu.VMEM((channels, sources, half), BF16),
            pltpu.VMEM((sources, channels, half), BF16),
            pltpu.VMEM((count * run, half, half), BF16),
            pltpu.VMEM((2, 2 * half, 2 * half), BF16),
            pltpu.VMEM((count, halves + 1, padded, half), F32),
            pltpu.SemaphoreType.DMA((5,)),
            pltpu.SemaphoreType.DMA((len(cuts) - 1,)),
        ],
        compiler_params=pltpu.CompilerParams(vmem_limit_bytes=VMEM_LIMIT),
        name="remap",
    )(live_count, *operands, *after)


def add_halves(kept, arrived, after=()):
    rows = kept.shape[0] // 2

    def kernel(kept_ref, arrived_ref, *refs):
        here_ref, there_ref = refs[len(after) :]
        here_ref[...] = kept_ref[:rows] + arrived_ref[:rows].astype(F32)
        there_ref[...] = (kept_ref[rows:] + arrived_ref[rows:].astype(F32)).astype(BF16)

    vmem = pl.BlockSpec(memory_space=pltpu.VMEM)
    return pl.pallas_call(
        kernel,
        in_specs=[vmem] * 2 + [pl.BlockSpec(memory_space=pl.ANY)] * len(after),
        out_specs=[vmem] * 2,
        out_shape=[
            jax.ShapeDtypeStruct((rows, kept.shape[1]), F32),
            jax.ShapeDtypeStruct((rows, kept.shape[1]), BF16),
        ],
        compiler_params=pltpu.CompilerParams(vmem_limit_bytes=VMEM_LIMIT),
        name="add_halves",
    )(kept, arrived, *after)


def sum_parts(parts, edge_rows):
    def kernel(*refs):
        total = refs[0][...].astype(F32)
        for ref in refs[1:-2]:
            total = total + ref[...].astype(F32)
        total = total.astype(BF16)
        refs[-2][...] = total
        refs[-1][...] = total[:edge_rows]

    return pl.pallas_call(
        kernel,
        out_shape=[
            jax.ShapeDtypeStruct(parts[0].shape, BF16),
            jax.ShapeDtypeStruct((edge_rows, parts[0].shape[1]), BF16),
        ],
        compiler_params=pltpu.CompilerParams(vmem_limit_bytes=VMEM_LIMIT),
        name="sum_parts",
    )(*parts)


def split_rows(padded):
    full = 16 * (padded // 16)
    return full, 16 * ((TAPS * (padded - full) + 15) // 16)


def prepare(conv_weight, nbr_block, nbr_code, padded, after):
    taps, channels, hidden = conv_weight.shape
    blocks = nbr_block.shape[0]
    pairs = (blocks + 1) // 2
    devices = lax.axis_size(("tile", "chan"))
    span = 2 * SIDE * pairs
    columns = 4 * 3 * span
    slots = blocks * 4 * SIDE
    full, rest = split_rows(padded)

    def kernel(nbr, code, taps_ref, unread, weight_ref, rim_ref, pick_ref):
        me = lax.axis_index(("tile", "chan"))
        empty = jnp.zeros((padded - channels, hidden), F32)
        rows = []
        for tap in range(taps):
            rows.append(jnp.concatenate([taps_ref[tap].astype(F32), empty], axis=0))
        tail = jnp.zeros((rest - taps * (padded - full), hidden), F32)
        stacked = [row[:full] for row in rows] + [row[full:] for row in rows] + [tail]
        weight_ref[...] = jnp.concatenate(stacked, axis=0).T.astype(BF16)
        for side in range(4):
            chosen = [rows[tap] for tap in rim_taps(side)]
            rim_ref[side * hidden : (side + 1) * hidden] = (
                jnp.concatenate(chosen, axis=0).T.astype(BF16)
            )
        lane = lax.broadcasted_iota(jnp.int32, (1, slots), 1)
        which = lane // SIDE
        position = lane % SIDE
        start = jnp.zeros((1, slots), jnp.int32)
        turned = jnp.zeros((1, slots), jnp.int32)
        for block in range(blocks):
            for side in range(4):
                other = nbr[side, block]
                turn = code[side, block]
                relative = lax.rem(other // blocks - me + 1 + devices, devices)
                column = (turn // 2 * 3 + relative) * span + lax.rem(other, blocks) * SIDE
                start = jnp.where(which == 4 * block + side, column, start)
                turned = jnp.where(which == 4 * block + side, turn % 2, turned)
        source = start + jnp.where(turned == 1, SIDE - 1 - position, position)
        row = lax.broadcasted_iota(jnp.int32, (columns, slots), 0)
        pick_ref[...] = jnp.where(row == source, 1.0, 0.0).astype(BF16)

    smem = pl.BlockSpec(memory_space=pltpu.SMEM)
    vmem = pl.BlockSpec(memory_space=pltpu.VMEM)
    return pl.pallas_call(
        kernel,
        in_specs=[smem, smem, vmem, pl.BlockSpec(memory_space=pl.ANY)],
        out_specs=[vmem] * 3,
        out_shape=[
            jax.ShapeDtypeStruct((hidden, taps * full + rest), BF16),
            jax.ShapeDtypeStruct((4 * hidden, 3 * padded), BF16),
            jax.ShapeDtypeStruct((columns, slots), BF16),
        ],
        compiler_params=pltpu.CompilerParams(vmem_limit_bytes=VMEM_LIMIT),
        name="prepare",
    )(nbr_block.T, nbr_code.T, conv_weight, after)


def incoming_rims(edges, rim_weight, pick, blocks, padded):
    pairs = (blocks + 1) // 2
    span = 2 * SIDE * pairs
    hidden = rim_weight.shape[0] // 4
    slots = pick.shape[1]

    def kernel(before_ref, own_ref, after_ref, weight_ref, pick_ref, edge_ref, out_ref):
        rows = []
        for ref in (before_ref, own_ref, after_ref):
            edges = ref[...].astype(F32)
            rows.append(
                jnp.concatenate(
                    [edges[pair * padded : (pair + 1) * padded] for pair in range(pairs)], axis=1
                )
            )
        shifted = jnp.dot(
            jnp.concatenate(rows, axis=0).astype(BF16),
            edge_ref[...],
            preferred_element_type=F32,
        )
        total = jnp.zeros((hidden, slots), F32)
        for side in range(4):
            stack = jnp.concatenate(
                [
                    jnp.concatenate(
                        [
                            shifted[
                                device * padded : (device + 1) * padded,
                                (4 * shift + side) * span : (4 * shift + side + 1) * span,
                            ]
                            for device in range(3)
                        ],
                        axis=1,
                    )
                    for shift in range(3)
                ],
                axis=0,
            ).astype(BF16)
            rims = jnp.dot(
                weight_ref[side * hidden : (side + 1) * hidden],
                stack,
                preferred_element_type=F32,
            ).astype(BF16)
            total = total + jnp.dot(
                rims,
                pick_ref[side * 3 * span : (side + 1) * 3 * span],
                preferred_element_type=F32,
            )
        out_ref[...] = total.astype(BF16)

    return pl.pallas_call(
        kernel,
        out_shape=jax.ShapeDtypeStruct((hidden, slots), BF16),
        compiler_params=pltpu.CompilerParams(vmem_limit_bytes=VMEM_LIMIT),
        name="rims",
    )(*edges, rim_weight, pick, constant(edge_matrix(pairs)))


def convolve(pieces, weight, incoming, blocks, padded):
    hidden = weight.shape[0]
    flat = [part for piece in pieces for part in piece]
    parts = len(flat)
    full, rest = split_rows(padded)
    evens, odds = (blocks + 1) // 2, blocks // 2
    order = [*range(0, blocks, 2), *range(1, blocks, 2)]

    def kernel(*refs):
        part_refs = list(refs[:parts])
        weight_ref, incoming_ref, shift_ref, place_ref = refs[parts : 4 + parts]
        out_ref, stack, result, sems = refs[4 + parts :]
        copies = []
        totals = []
        for piece in pieces:
            total = part_refs.pop(0)[...].astype(F32)
            for _ in piece[1:]:
                total = total + part_refs.pop(0)[...].astype(F32)
            totals.append(total)
        total = jnp.concatenate(totals, axis=0)
        edge_rows, both = evens * padded, odds * padded
        edge, middle = total[:both], total[edge_rows : edge_rows + both]
        lane = lax.broadcasted_iota(jnp.int32, (both, LANES), 1)
        even = jnp.where(lane < 64, edge, middle)
        odd = pltpu.roll(jnp.where(lane < 64, middle, edge), 64, 1)
        lead = jnp.concatenate([even, total[both:edge_rows], odd], axis=0)
        cells = jnp.concatenate([lead, total[edge_rows + both :]], axis=1).astype(BF16)
        rests = []
        for tap in range(TAPS):
            moved = jnp.dot(cells, shift_ref[tap], preferred_element_type=F32)
            moved = moved.reshape(blocks, padded, CELLS)
            stack[:, full * tap : full * (tap + 1), :] = moved[:, :full].astype(BF16)
            rests.append(moved[:, full:])
        rests.append(jnp.zeros((blocks, rest - TAPS * (padded - full), CELLS), F32))
        stack[:, full * TAPS :, :] = jnp.concatenate(rests, axis=1).astype(BF16)
        for index, block in enumerate(order):
            grad = jnp.dot(
                weight_ref[...], stack[index], preferred_element_type=F32
            ) + jnp.dot(
                incoming_ref[:, 64 * block : 64 * (block + 1)],
                place_ref[...],
                preferred_element_type=F32,
            )
            result[block] = grad.astype(BF16)
            copies.append(
                pltpu.make_async_copy(result.at[block], out_ref.at[block], sems.at[block])
            )
            copies[-1].start()
        for copy in copies:
            copy.wait()

    return pl.pallas_call(
        kernel,
        out_shape=jax.ShapeDtypeStruct((blocks, hidden, CELLS), BF16),
        out_specs=pl.BlockSpec(memory_space=pltpu.HBM),
        scratch_shapes=[
            pltpu.VMEM((blocks, TAPS * full + rest, CELLS), BF16),
            pltpu.VMEM((blocks, hidden, CELLS), BF16),
            pltpu.SemaphoreType.DMA((blocks,)),
        ],
        compiler_params=pltpu.CompilerParams(vmem_limit_bytes=VMEM_LIMIT),
        name="convolve",
    )(
        *flat,
        weight,
        incoming,
        constant(shift_matrices()),
        constant(place_matrix()),
    )


def from_behind(value, axis, steps):
    count = lax.axis_size(axis)
    pairs = [(source, (source + steps) % count) for source in range(count)]
    return lax.ppermute(value, axis, pairs)


def swapped(value, flip):
    pairs = [(source, source ^ flip) for source in range(lax.axis_size("tile"))]
    return lax.ppermute(value, "tile", pairs)


def summed_here(
    prepare, latlon_grad, remap_weight, src_block, owner, target_half, live_count, blocks, padded
):
    operands = (
        latlon_grad, remap_weight, src_block, owner, target_half, live_count, blocks, padded
    )
    moving = list(remap_runs((1, 3), BF16, *operands))
    kept = remap_runs((0, 2), F32, *operands, (moving[0],))
    ready = prepare(kept[0])
    pieces = []
    for index, stays in enumerate(kept):
        arrives = swapped(moving[index], 1)
        stays, leaves = add_halves(stays, arrives, ())
        pieces.append([stays, swapped(leaves, 2)])
    return pieces, ready


def summed_there(
    prepare, latlon_grad, remap_weight, src_block, owner, target_half, live_count, blocks, padded
):
    slots, half = remap_weight.shape[:2]
    channels = latlon_grad.shape[1]
    tiles = lax.axis_size("tile")
    run = slots // tiles
    live = jnp.arange(slots, dtype=jnp.int32) < live_count[0]
    runs = jnp.argsort(owner.reshape(tiles, run)[:, 0])
    picked = jnp.take(latlon_grad, src_block, axis=0)
    product = jnp.einsum("eoa,eab->eob", picked, remap_weight, preferred_element_type=F32)
    product = jnp.where(live[:, None, None], product, 0).astype(BF16)
    outgoing = jnp.take(product.reshape(tiles, run, channels, half), runs, axis=0)
    ids = jnp.take(target_half.reshape(tiles, run), runs, axis=0)
    arrived = lax.all_to_all(outgoing, "tile", split_axis=0, concat_axis=0, tiled=True)
    ids = lax.all_to_all(ids, "tile", split_axis=0, concat_axis=0, tiled=True).reshape(slots)
    selector = (jnp.arange(2 * blocks, dtype=jnp.int32)[:, None] == ids[None, :]).astype(BF16)
    sums = jnp.einsum(
        "hs,soa->hoa",
        selector,
        arrived.reshape(slots, channels, half),
        preferred_element_type=F32,
    ).astype(BF16)
    cells = sums.reshape(blocks, 2, channels, half).transpose(0, 2, 1, 3)
    cells = cells.reshape(blocks, channels, 2 * half)[:, :, np.array(lane_order())]
    cells = jnp.pad(cells, ((0, 0), (0, padded - channels), (0, 0)))
    even, odd = cells[0::2], cells[1::2]
    count = blocks // 2
    edges = jnp.concatenate([even[:count, :, :64], odd[:, :, :64]], axis=2)
    middle = jnp.concatenate([odd[:, :, 64:128], even[:count, :, 64:128]], axis=2)
    rows = jnp.concatenate(
        [edges, even[count:, :, :128], middle, even[:, :, 128:], odd[:, :, 128:]], axis=0
    )
    rows = rows.reshape(-1, half)
    pieces = [[rows[first:last]] for first, last in piece_rows(blocks, padded)]
    return pieces, prepare(rows)


def per_device(
    latlon_grad,
    remap_weight,
    src_block,
    owner,
    target_half,
    live_count,
    conv_weight,
    nbr_block,
    nbr_code,
):
    channels = latlon_grad.shape[1]
    hidden = conv_weight.shape[2]
    blocks = nbr_block.shape[0]
    padded = 8 * ((channels + 7) // 8)
    run = remap_weight.shape[0] // lax.axis_size("tile")
    small = lax.axis_size("tile") == 4 and run >= 2 * blocks
    gather = summed_here if small else summed_there
    ready = functools.partial(prepare, conv_weight, nbr_block, nbr_code, padded)
    pieces, (weight, rim_weight, pick) = gather(
        ready,
        latlon_grad,
        remap_weight,
        src_block,
        owner,
        target_half,
        live_count,
        blocks,
        padded,
    )
    lead, edges = sum_parts(pieces[0], (blocks + 1) // 2 * padded)
    pieces[0] = [lead]
    before = from_behind(edges, ("tile", "chan"), 1)
    after = from_behind(edges, ("tile", "chan"), -1)
    incoming = incoming_rims((before, edges, after), rim_weight, pick, blocks, padded)
    grads = convolve(pieces, weight, incoming, blocks, padded)
    return grads.transpose(1, 0, 2)


def solution(mesh):
    in_specs = (
        P(("member", "tile", "chan"), None, None),
        P(("tile", "chan"), None, None),
        P(("tile", "chan")),
        P(("tile", "chan")),
        P(("tile", "chan")),
        P(("tile", "chan")),
        P(),
        P(("tile", "chan"), None),
        P(("tile", "chan"), None),
    )
    out_specs = P(None, ("member", "tile", "chan"), None)
    return jax.shard_map(
        per_device, mesh=mesh, in_specs=in_specs, out_specs=out_specs, check_vma=False
    )
```

time: 41.5 us -> 35 us (0.84)
  waiting for transfers between devices: 8.56 us -> 2.81 us
  starting transfers between devices: 12.4 us -> 16.1 us
  Pallas kernels: 18.6 us -> 15.1 us
  local copies, waits for them, and re-layouts: 0.93 us -> 0.04 us
    ppermute x0 -> x6, starting transfers between devices: none -> 11.6 us  [swapped(): return lax.ppermute(value, 'tile', pairs)]
    ppermute x8 -> x2, waiting for transfers between devices: 8.56 us -> 0.01 us  [from_behind(): return lax.ppermute(value, axis, pairs)]
    ppermute x8 -> x2, starting transfers between devices: 12.4 us -> 4.49 us  [from_behind(): return lax.ppermute(value, axis, pairs)]
    ppermute x0 -> x6, waiting for transfers between devices: none -> 2.8 us  [swapped(): return lax.ppermute(value, 'tile', pairs)]
    pallas_call x2, Pallas kernels: 10.7 us -> 8.8 us  [remap_runs(): pl.pallas_call(kernel, in_specs=[pl.BlockSpec(memory_space=pltpu.SMEM)] +...]
    unnamed x14 -> x12, local copies, waits for them, and re-layouts: 0.93 us -> 0.04 us
    pallas_call x1, Pallas kernels: 2.5 us -> 1.68 us  [incoming_rims(): pl.pallas_call(kernel, out_shape=jax.ShapeDtypeStruct((hidden, slots), BF...]
    pallas_call x1, Pallas kernels: 3.34 us -> 2.57 us  [convolve(): pl.pallas_call(kernel, out_shape=jax.ShapeDtypeStruct((blocks, hidden, CE...]
  transfers between devices with their start and end apart: 8 -> 8, of which waited for: 4 -> 3; matrix products, arithmetic and copies ran while one was open for 0% -> 0% of each run, Pallas kernels for 29% -> 23%
where the time goes in v1:
time: 35 us; the launch traced here: 34.8 us
  starting transfers between devices  16.1 us (46%)
  Pallas kernels  15.1 us (43%)
  waiting for transfers between devices  2.81 us (8%)
  between operations  0.78 us (2%)
    ppermute x6, starting transfers between devices, swapped(): return lax.ppermute(value, 'tile', pairs)  11.6 us
    pallas_call x2, Pallas kernels, remap_runs(): pl.pallas_call(kernel, in_specs=[pl.BlockSpec(memory_space=pltpu.SMEM)] +...  8.8 us
    ppermute x2, starting transfers between devices, from_behind(): return lax.ppermute(value, axis, pairs)  4.49 us
    ppermute x6, waiting for transfers between devices, swapped(): return lax.ppermute(value, 'tile', pairs)  2.8 us
    pallas_call x1, Pallas kernels, convolve(): pl.pallas_call(kernel, out_shape=jax.ShapeDtypeStruct((blocks, hidden, CE...  2.57 us
    pallas_call x1, Pallas kernels, prepare(): pl.pallas_call(kernel, in_specs=[smem, smem, vmem, pl.BlockSpec(memory_sp...  1.89 us
    pallas_call x1, Pallas kernels, incoming_rims(): pl.pallas_call(kernel, out_shape=jax.ShapeDtypeStruct((hidden, slots), BF...  1.68 us
  transfers between devices with their start and end apart: 8, of which 3 were waited for; matrix products, arithmetic and copies ran while one was open for 0% of the time, Pallas kernels for 23%

profile of v1, /device:TPU:0, one launch (start us, length us, event | category | flops | bytes accessed | tf_op | source)
XLA Modules:
  0.0 34.8 jit_solution(5805180806162597068)
XLA Ops:
  0.7 4.3 %remap.2 = (bf16[720,128]{1,0:T(8,128)(2,1)S(1)}, bf16[720,128]{1,0:T(8,128)(2,1)S(1)}, bf16[576,128]{1,0:T(8,128)(2,1)S(1)}) custom-call(s32[1]{0:T(128)S(6)} %copy.15.refs_0_, s32[256]{0:T(256)} %refs_1_.3, s32[256]{0:T(256)} %refs_2_.3, s32[256]{0:T(256)} %refs_3_.3, bf16[69,4,128]{2,1,0:T(4,128)(2,1)} %bitcast.6, bf16[256,128,128]{2,1,0:T(8,128)(2,1)} %refs_5_.3, ...), custom_call_target="tpu_custom_call" | custom-call | tf_op jit(solution)/shard_map/remap/pallas_call | solution.py:230
  5.0 3.2 %collective-permute-start = (bf16[720,128]{1,0:T(8,128)(2,1)S(1)}, bf16[720,128]{1,0:T(8,128)(2,1)S(1)}, u32[]{:S(2)}, u32[]{:S(2)}) collective-permute-start(bf16[720,128]{1,0:T(8,128)(2,1)S(1)} %get-tuple-element.22.refs_7_), channel_id=1, source_target_pairs={{0,4},{4,0},{8,12},{12,8},{1,5},{5,1},{9,13},{13,9},{2,6},{6,2},{1... | collective-permute-start | bytes 552968 | tf_op jit(solution)/shard_map/ppermute | solution.py:497
  8.1 0.1 collective-permute-start.2
  8.2 1.9 %collective-permute-start.4 = (bf16[576,128]{1,0:T(8,128)(2,1)S(1)}, bf16[576,128]{1,0:T(8,128)(2,1)S(1)}, u32[]{:S(2)}, u32[]{:S(2)}) collective-permute-start(bf16[576,128]{1,0:T(8,128)(2,1)S(1)} %get-tuple-element.32), channel_id=1, source_target_pairs={{0,4},{4,0},{8,12},{12,8},{1,5},{5,1},{9,13},{13,9},{2,6},{6,2},{1... | collective-permute-start | bytes 442376 | tf_op jit(solution)/shard_map/ppermute | solution.py:497
  10.2 4.5 %remap.3 = (f32[720,128]{1,0:T(8,128)S(1)}, f32[720,128]{1,0:T(8,128)S(1)}, f32[576,128]{1,0:T(8,128)S(1)}) custom-call(s32[1]{0:T(128)S(6)} %copy.15.refs_0_, s32[256]{0:T(256)} %refs_1_.3, s32[256]{0:T(256)} %refs_2_.3, s32[256]{0:T(256)} %refs_3_.3, bf16[69,4,128]{2,1,0:T(4,128)(2,1)} %bitcast.7, bf16[256,128,128]{2,1,0:T(8,128)(2,1)} %refs_5_.3, ...), custom_call_target="tpu_custom_call" | custom-call | tf_op jit(solution)/shard_map/remap/pallas_call | solution.py:230
  14.7 0.0 copy-start.4
  14.7 0.0 copy-start.5
  14.7 0.0 copy-start
  14.8 2.7 %collective-permute-start.1 = (bf16[360,128]{1,0:T(8,128)(2,1)S(1)}, bf16[360,128]{1,0:T(8,128)(2,1)S(1)}, u32[]{:S(2)}, u32[]{:S(2)}) collective-permute-start(bf16[360,128]{1,0:T(8,128)(2,1)S(1)} %get-tuple-element.25), channel_id=1, source_target_pairs={{0,8},{4,12},{8,0},{12,4},{1,9},{5,13},{9,1},{13,5},{2,10},{6,14},... | collective-permute-start | bytes 276488 | tf_op jit(solution)/shard_map/ppermute | solution.py:497
  17.4 1.1 %collective-permute-done.2.arrived_ref = bf16[720,128]{1,0:T(8,128)(2,1)S(1)} collective-permute-done((bf16[720,128]{1,0:T(8,128)(2,1)S(1)}, bf16[720,128]{1,0:T(8,128)(2,1)S(1)}, u32[]{:S(2)}, u32[]{:S(2)}) %collective-permute-start.2) | collective-permute-done | bytes 184352 | tf_op jit(solution)/shard_map/ppermute | solution.py:497
  18.6 2.1 %collective-permute-start.3 = (bf16[360,128]{1,0:T(8,128)(2,1)S(1)}, bf16[360,128]{1,0:T(8,128)(2,1)S(1)}, u32[]{:S(2)}, u32[]{:S(2)}) collective-permute-start(bf16[360,128]{1,0:T(8,128)(2,1)S(1)} %get-tuple-element.30), channel_id=1, source_target_pairs={{0,8},{4,12},{8,0},{12,4},{1,9},{5,13},{9,1},{13,5},{2,10},{6,14},... | collective-permute-start | bytes 276488 | tf_op jit(solution)/shard_map/ppermute | solution.py:497
  20.7 1.5 %collective-permute-done.1.refs_1_ = bf16[360,128]{1,0:T(8,128)(2,1)S(1)} collective-permute-done((bf16[360,128]{1,0:T(8,128)(2,1)S(1)}, bf16[360,128]{1,0:T(8,128)(2,1)S(1)}, u32[]{:S(2)}, u32[]{:S(2)}) %collective-permute-start.1) | collective-permute-done | bytes 92192 | tf_op jit(solution)/shard_map/ppermute | solution.py:497
  22.2 0.1 collective-permute-start.6
  22.3 4.4 %collective-permute-start.7 = (bf16[288,128]{1,0:T(8,128)(2,1)S(1)}, bf16[288,128]{1,0:T(8,128)(2,1)S(1)}, u32[]{:S(2)}, u32[]{:S(2)}) collective-permute-start(bf16[288,128]{1,0:T(8,128)(2,1)S(1)} %get-tuple-element.36.own_ref), channel_id=1, source_target_pairs={{0,15},{1,0},{2,1},{3,2},{4,3},{5,4},{6,5},{7,6},{8,7},{9,8},{10,9... | collective-permute-start | bytes 221192 | tf_op jit(solution)/shard_map/ppermute | solution.py:492
  26.7 0.0 collective-permute-done.4.arrived_ref
  26.7 1.7 %collective-permute-start.5 = (bf16[288,128]{1,0:T(8,128)(2,1)S(1)}, bf16[288,128]{1,0:T(8,128)(2,1)S(1)}, u32[]{:S(2)}, u32[]{:S(2)}) collective-permute-start(bf16[288,128]{1,0:T(8,128)(2,1)S(1)} %get-tuple-element.34), channel_id=1, source_target_pairs={{0,8},{4,12},{8,0},{12,4},{1,9},{5,13},{9,1},{13,5},{2,10},{6,14},... | collective-permute-start | bytes 221192 | tf_op jit(solution)/shard_map/ppermute | solution.py:497
  28.4 1.9 %prepare.1 = (bf16[256,656]{1,0:T(8,128)(2,1)S(1)}, bf16[1024,216]{1,0:T(8,128)(2,1)S(1)}, bf16[1536,448]{1,0:T(8,128)(2,1)S(1)}) custom-call(s32[4,7]{1,0:T(4,128)S(1)} %bitcast.4, s32[4,7]{1,0:T(4,128)S(1)} %bitcast.5, bf16[9,69,256]{2,1,0:T(8,128)(2,1)S(1)} %copy-done.2, f32[720,128]{1,0:T(8,128)S(1)} %get-tuple-element.23.kept_ref.unread), custom_call_target="tpu_custom_call" | custom-call | tf_op jit(solution)/shard_map/prepare/pallas_call | solution.py:346
  30.3 0.0 collective-permute-done.6.before_ref
  30.4 0.0 copy-start.1
  30.4 0.0 copy-start.3
  30.4 1.7 %rims.1.refs_6_ = bf16[256,448]{1,0:T(8,128)(2,1)S(1)} custom-call(bf16[288,128]{1,0:T(8,128)(2,1)S(1)} %collective-permute-done.6.before_ref, bf16[288,128]{1,0:T(8,128)(2,1)S(1)} %get-tuple-element.36.own_ref, bf16[288,128]{1,0:T(8,128)(2,1)S(1)} %collective-permute-done.7.after_ref, bf16[1024,216]{1,0:T(8,128)(2,1)S(1)} %get-tuple-element.37.weight_ref, ...), custom_call_target="tpu_custom_call" | custom-call | tf_op jit(solution)/shard_map/rims/pallas_call | solution.py:410
  32.1 0.2 collective-permute-done.5.refs_4_
  32.2 0.0 collective-permute-done.3.refs_2_
  32.2 2.6 %convolve.1 = bf16[7,256,256]{2,1,0:T(8,128)(2,1)} custom-call(bf16[360,128]{1,0:T(8,128)(2,1)S(1)} %get-tuple-element.26.refs_0_, f32[360,128]{1,0:T(8,128)S(1)} %get-tuple-element.29.refs_1_, bf16[360,128]{1,0:T(8,128)(2,1)S(1)} %collective-permute-done.3.refs_2_, f32[288,128]{1,0:T(8,128)S(1)} %get-tuple-element.33.refs_3_, ...), custom_call_target="tpu_custom_call" | custom-call | tf_op jit(solution)/shard_map/convolve/pallas_call | solution.py:469
  (13 shorter events, 0.2 us)
Async XLA Ops:
  5.0 9.7 %collective-permute-start = (bf16[720,128]{1,0:T(8,128)(2,1)S(1)}, bf16[720,128]{1,0:T(8,128)(2,1)S(1)}, u32[]{:S(2)}, u32[]{:S(2)}) collective-permute-start(bf16[720,128]{1,0:T(8,128)(2,1)S(1)} %get-tuple-element.22.refs_7_), channel_id=1, source_target_pairs={{0,4},{4,0},{8,12},{12,8},{1,5},{5,1},{9,13},{13,9},{2,6},{6,2},{1... | collective-permute-start | bytes 552968 | tf_op jit(solution)/shard_map/ppermute | solution.py:497
  8.1 10.4 %collective-permute-start.2 = (bf16[720,128]{1,0:T(8,128)(2,1)S(1)}, bf16[720,128]{1,0:T(8,128)(2,1)S(1)}, u32[]{:S(2)}, u32[]{:S(2)}) collective-permute-start(bf16[720,128]{1,0:T(8,128)(2,1)S(1)} %get-tuple-element.28), channel_id=1, source_target_pairs={{0,4},{4,0},{8,12},{12,8},{1,5},{5,1},{9,13},{13,9},{2,6},{6,2},{1... | collective-permute-start | bytes 552968 | tf_op jit(solution)/shard_map/ppermute | solution.py:497
  8.2 18.5 %collective-permute-start.4 = (bf16[576,128]{1,0:T(8,128)(2,1)S(1)}, bf16[576,128]{1,0:T(8,128)(2,1)S(1)}, u32[]{:S(2)}, u32[]{:S(2)}) collective-permute-start(bf16[576,128]{1,0:T(8,128)(2,1)S(1)} %get-tuple-element.32), channel_id=1, source_target_pairs={{0,4},{4,0},{8,12},{12,8},{1,5},{5,1},{9,13},{13,9},{2,6},{6,2},{1... | collective-permute-start | bytes 442376 | tf_op jit(solution)/shard_map/ppermute | solution.py:497
  10.2 18.3 %copy-start.2 = (bf16[9,69,256]{2,1,0:T(8,128)(2,1)S(1)}, bf16[9,69,256]{2,1,0:T(8,128)(2,1)}, u32[]{:S(2)}) copy-start(bf16[9,69,256]{2,1,0:T(8,128)(2,1)} %taps_ref.1) | copy-start | bytes 953860
  14.7 13.8 %copy-start.4 = (s32[7,4]{0,1:T(4,128)S(1)}, s32[7,4]{0,1:T(4,128)}, u32[]{:S(2)}) copy-start(s32[7,4]{0,1:T(4,128)} %param.21) | copy-start | bytes 340
  14.7 13.8 %copy-start.5 = (s32[7,4]{0,1:T(4,128)S(1)}, s32[7,4]{0,1:T(4,128)}, u32[]{:S(2)}) copy-start(s32[7,4]{0,1:T(4,128)} %param.22) | copy-start | bytes 340
  14.7 15.7 %copy-start = (bf16[512,1536]{1,0:T(8,128)(2,1)S(1)}, bf16[512,1536]{1,0:T(8,128)(2,1)}, u32[]{:S(2)}) copy-start(bf16[512,1536]{1,0:T(8,128)(2,1)} %constant.9.clone.edge_ref) | copy-start | bytes 4718596
  14.8 7.4 %collective-permute-start.1 = (bf16[360,128]{1,0:T(8,128)(2,1)S(1)}, bf16[360,128]{1,0:T(8,128)(2,1)S(1)}, u32[]{:S(2)}, u32[]{:S(2)}) collective-permute-start(bf16[360,128]{1,0:T(8,128)(2,1)S(1)} %get-tuple-element.25), channel_id=1, source_target_pairs={{0,8},{4,12},{8,0},{12,4},{1,9},{5,13},{9,1},{13,5},{2,10},{6,14},... | collective-permute-start | bytes 276488 | tf_op jit(solution)/shard_map/ppermute | solution.py:497
  18.6 13.6 %collective-permute-start.3 = (bf16[360,128]{1,0:T(8,128)(2,1)S(1)}, bf16[360,128]{1,0:T(8,128)(2,1)S(1)}, u32[]{:S(2)}, u32[]{:S(2)}) collective-permute-start(bf16[360,128]{1,0:T(8,128)(2,1)S(1)} %get-tuple-element.30), channel_id=1, source_target_pairs={{0,8},{4,12},{8,0},{12,4},{1,9},{5,13},{9,1},{13,5},{2,10},{6,14},... | collective-permute-start | bytes 276488 | tf_op jit(solution)/shard_map/ppermute | solution.py:497
  22.2 8.1 %collective-permute-start.6 = (bf16[288,128]{1,0:T(8,128)(2,1)S(1)}, bf16[288,128]{1,0:T(8,128)(2,1)S(1)}, u32[]{:S(2)}, u32[]{:S(2)}) collective-permute-start(bf16[288,128]{1,0:T(8,128)(2,1)S(1)} %get-tuple-element.36.own_ref), channel_id=1, source_target_pairs={{0,1},{1,2},{2,3},{3,4},{4,5},{5,6},{6,7},{7,8},{8,9},{9,10},{10,1... | collective-permute-start | bytes 221192 | tf_op jit(solution)/shard_map/ppermute | solution.py:492
  22.3 8.1 %collective-permute-start.7 = (bf16[288,128]{1,0:T(8,128)(2,1)S(1)}, bf16[288,128]{1,0:T(8,128)(2,1)S(1)}, u32[]{:S(2)}, u32[]{:S(2)}) collective-permute-start(bf16[288,128]{1,0:T(8,128)(2,1)S(1)} %get-tuple-element.36.own_ref), channel_id=1, source_target_pairs={{0,15},{1,0},{2,1},{3,2},{4,3},{5,4},{6,5},{7,6},{8,7},{9,8},{10,9... | collective-permute-start | bytes 221192 | tf_op jit(solution)/shard_map/ppermute | solution.py:492
  26.7 5.5 %collective-permute-start.5 = (bf16[288,128]{1,0:T(8,128)(2,1)S(1)}, bf16[288,128]{1,0:T(8,128)(2,1)S(1)}, u32[]{:S(2)}, u32[]{:S(2)}) collective-permute-start(bf16[288,128]{1,0:T(8,128)(2,1)S(1)} %get-tuple-element.34), channel_id=1, source_target_pairs={{0,8},{4,12},{8,0},{12,4},{1,9},{5,13},{9,1},{13,5},{2,10},{6,14},... | collective-permute-start | bytes 221192 | tf_op jit(solution)/shard_map/ppermute | solution.py:497
  30.4 1.9 %copy-start.1 = (bf16[9,256,256]{2,1,0:T(8,128)(2,1)S(1)}, bf16[9,256,256]{2,1,0:T(8,128)(2,1)}, u32[]{:S(2)}) copy-start(bf16[9,256,256]{2,1,0:T(8,128)(2,1)} %constant.10.clone.refs_7_) | copy-start | bytes 3538948
  30.4 1.9 %copy-start.3 = (bf16[64,256]{1,0:T(8,128)(2,1)S(1)}, bf16[64,256]{1,0:T(8,128)(2,1)}, u32[]{:S(2)}) copy-start(bf16[64,256]{1,0:T(8,128)(2,1)} %constant.11.clone.refs_8_) | copy-start | bytes 98308

commit v2 on v1

--- a/solution.py
+++ b/solution.py
@@ -15,7 +15,7 @@
 LANES = 128
 TAPS = 9
 VMEM_LIMIT = 48 * 1024 * 1024
-PIECES = 3
+SHARES = (6, 5, 3)
 
 
 def edge_cell(side, position):
@@ -96,7 +96,8 @@
 
 def piece_rows(blocks, padded):
     tiles = 2 * blocks
-    cuts = [-(-tiles * index // PIECES) for index in range(PIECES + 1)]
+    shares = [sum(SHARES[:index]) for index in range(len(SHARES) + 1)]
+    cuts = [-(-tiles * share // shares[-1]) for share in shares]
     cuts[1] = max(cuts[1], (blocks + 1) // 2)
     return [(first * padded, last * padded) for first, last in zip(cuts[:-1], cuts[1:])]
 
@@ -173,7 +174,8 @@
             grad[source] = wide[:, source].astype(BF16)
         lane = lax.broadcasted_iota(jnp.int32, (odds * padded, half), 1)
         for part, (start, stop) in enumerate(zip(cuts[:-1], cuts[1:])):
-            large[part].wait()
+            if part == 0 or start % run:
+                large[part].wait()
             index = start // run
             for slot in range(start, stop):
                 entry = firsts[index] + slot % run
@@ -185,6 +187,8 @@
                 continue
             if index == 0:
                 small[4].wait()
+            if index + 1 < count:
+                large[part + 1].wait()
             moved = []
             for parity in range(2):
                 joined = jnp.concatenate(
@@ -334,7 +338,8 @@
                 other = nbr[side, block]
                 turn = code[side, block]
                 relative = lax.rem(other // blocks - me + 1 + devices, devices)
-                column = (turn // 2 * 3 + relative) * span + lax.rem(other, blocks) * SIDE
+                part = relative
+                column = (turn // 2 * 3 + part) * span + lax.rem(other, blocks) * SIDE
                 start = jnp.where(which == 4 * block + side, column, start)
                 turned = jnp.where(which == 4 * block + side, turn % 2, turned)
         source = start + jnp.where(turned == 1, SIDE - 1 - position, position)
@@ -363,9 +368,9 @@
     hidden = rim_weight.shape[0] // 4
     slots = pick.shape[1]
 
-    def kernel(before_ref, own_ref, after_ref, weight_ref, pick_ref, edge_ref, out_ref):
+    def kernel(near_ref, own_ref, far_ref, weight_ref, pick_ref, edge_ref, out_ref):
         rows = []
-        for ref in (before_ref, own_ref, after_ref):
+        for ref in (near_ref, own_ref, far_ref):
             edges = ref[...].astype(F32)
             rows.append(
                 jnp.concatenate(
@@ -377,7 +382,7 @@
             edge_ref[...],
             preferred_element_type=F32,
         )
-        total = jnp.zeros((hidden, slots), F32)
+        rims = []
         for side in range(4):
             stack = jnp.concatenate(
                 [
@@ -395,17 +400,16 @@
                 ],
                 axis=0,
             ).astype(BF16)
-            rims = jnp.dot(
-                weight_ref[side * hidden : (side + 1) * hidden],
-                stack,
-                preferred_element_type=F32,
-            ).astype(BF16)
-            total = total + jnp.dot(
-                rims,
-                pick_ref[side * 3 * span : (side + 1) * 3 * span],
-                preferred_element_type=F32,
-            )
-        out_ref[...] = total.astype(BF16)
+            rims.append(
+                jnp.dot(
+                    weight_ref[side * hidden : (side + 1) * hidden],
+                    stack,
+                    preferred_element_type=F32,
+                ).astype(BF16)
+            )
+        out_ref[...] = jnp.dot(
+            jnp.concatenate(rims, axis=1), pick_ref[...], preferred_element_type=F32
+        ).astype(BF16)
 
     return pl.pallas_call(
         kernel,
@@ -486,12 +490,6 @@
     )
 
 
-def from_behind(value, axis, steps):
-    count = lax.axis_size(axis)
-    pairs = [(source, (source + steps) % count) for source in range(count)]
-    return lax.ppermute(value, axis, pairs)
-
-
 def swapped(value, flip):
     pairs = [(source, source ^ flip) for source in range(lax.axis_size("tile"))]
     return lax.ppermute(value, "tile", pairs)
@@ -505,13 +503,14 @@
     )
     moving = list(remap_runs((1, 3), BF16, *operands))
     kept = remap_runs((0, 2), F32, *operands, (moving[0],))
-    ready = prepare(kept[0])
     pieces = []
     for index, stays in enumerate(kept):
-        arrives = swapped(moving[index], 1)
-        stays, leaves = add_halves(stays, arrives, ())
+        stays, leaves = add_halves(stays, swapped(moving[index], 1))
+        if index == 0:
+            weight, *ready = prepare(leaves)
+            weight, moving[-1] = lax.optimization_barrier((weight, moving[-1]))
         pieces.append([stays, swapped(leaves, 2)])
-    return pieces, ready
+    return pieces, (weight, *ready)
 
 
 def summed_there(
@@ -584,9 +583,13 @@
     )
     lead, edges = sum_parts(pieces[0], (blocks + 1) // 2 * padded)
     pieces[0] = [lead]
-    before = from_behind(edges, ("tile", "chan"), 1)
-    after = from_behind(edges, ("tile", "chan"), -1)
-    incoming = incoming_rims((before, edges, after), rim_weight, pick, blocks, padded)
+    count = lax.axis_size(("tile", "chan"))
+    near = [(source, (source + 1) % count) for source in range(count)]
+    far = [(source, (source - 1) % count) for source in range(count)]
+    arrived = [lax.ppermute(edges, ("tile", "chan"), pairs) for pairs in (near, far)]
+    incoming = incoming_rims(
+        (arrived[0], edges, arrived[1]), rim_weight, pick, blocks, padded
+    )
     grads = convolve(pieces, weight, incoming, blocks, padded)
     return grads.transpose(1, 0, 2)
 

time: 35 us -> 33.9 us (0.969)
  starting transfers between devices: 16.1 us -> 13.9 us
  waiting for transfers between devices: 2.81 us -> 4.56 us
  Pallas kernels: 15.1 us -> 14.4 us
    ppermute x6, starting transfers between devices: 11.6 us -> 9.42 us  [swapped(): return lax.ppermute(value, 'tile', pairs)]
    ppermute x2, waiting for transfers between devices: 0.01 us -> 1.17 us  [per_device(): lax.ppermute(edges, ('tile', 'chan'), pairs)]
    ppermute x6, waiting for transfers between devices: 2.8 us -> 3.38 us  [swapped(): return lax.ppermute(value, 'tile', pairs)]
    pallas_call x1, Pallas kernels: 1.68 us -> 1.32 us  [incoming_rims(): pl.pallas_call(kernel, out_shape=jax.ShapeDtypeStruct((hidden, slots), BF...]
where the time goes in v2:
time: 33.9 us; the launch traced here: 33.7 us
  Pallas kernels  14.4 us (42%)
  starting transfers between devices  13.9 us (41%)
  waiting for transfers between devices  4.56 us (13%)
  between operations  0.74 us (2%)
    ppermute x6, starting transfers between devices, swapped(): return lax.ppermute(value, 'tile', pairs)  9.42 us
    pallas_call x2, Pallas kernels, remap_runs(): pl.pallas_call(kernel, in_specs=[pl.BlockSpec(memory_space=pltpu.SMEM)] +...  8.52 us
    ppermute x2, starting transfers between devices, per_device(): lax.ppermute(edges, ('tile', 'chan'), pairs)  4.49 us
    ppermute x6, waiting for transfers between devices, swapped(): return lax.ppermute(value, 'tile', pairs)  3.38 us
    pallas_call x1, Pallas kernels, convolve(): pl.pallas_call(kernel, out_shape=jax.ShapeDtypeStruct((blocks, hidden, CE...  2.56 us
    pallas_call x1, Pallas kernels, prepare(): pl.pallas_call(kernel, in_specs=[smem, smem, vmem, pl.BlockSpec(memory_sp...  1.89 us
    pallas_call x1, Pallas kernels, incoming_rims(): pl.pallas_call(kernel, out_shape=jax.ShapeDtypeStruct((hidden, slots), BF...  1.32 us
    ppermute x2, waiting for transfers between devices, per_device(): lax.ppermute(edges, ('tile', 'chan'), pairs)  1.17 us
  transfers between devices with their start and end apart: 8, of which 3 were waited for; matrix products, arithmetic and copies ran while one was open for 0% of the time, Pallas kernels for 23%

profile of v2, /device:TPU:0, one launch (start us, length us, event | category | flops | bytes accessed | tf_op | source)
XLA Modules:
  0.0 33.7 jit_solution(1377195757787651652)
XLA Ops:
  0.7 4.2 %remap.2 = (bf16[864,128]{1,0:T(8,128)(2,1)S(1)}, bf16[720,128]{1,0:T(8,128)(2,1)S(1)}, bf16[432,128]{1,0:T(8,128)(2,1)S(1)}) custom-call(s32[1]{0:T(128)S(6)} %copy.15.refs_0_, s32[256]{0:T(256)} %refs_1_.3, s32[256]{0:T(256)} %refs_2_.3, s32[256]{0:T(256)} %refs_3_.3, bf16[69,4,128]{2,1,0:T(4,128)(2,1)} %bitcast.6, bf16[256,128,128]{2,1,0:T(8,128)(2,1)} %refs_5_.3, ...), custom_call_target="tpu_custom_call" | custom-call | tf_op jit(solution)/shard_map/remap/pallas_call | solution.py:234
  4.9 3.1 %collective-permute-start = (bf16[864,128]{1,0:T(8,128)(2,1)S(1)}, bf16[864,128]{1,0:T(8,128)(2,1)S(1)}, u32[]{:S(2)}, u32[]{:S(2)}) collective-permute-start(bf16[864,128]{1,0:T(8,128)(2,1)S(1)} %get-tuple-element.24.refs_7_), channel_id=1, source_target_pairs={{0,4},{4,0},{8,12},{12,8},{1,5},{5,1},{9,13},{13,9},{2,6},{6,2},{1... | collective-permute-start | bytes 663560 | tf_op jit(solution)/shard_map/ppermute | solution.py:495
  8.0 0.1 collective-permute-start.2
  8.1 4.3 %remap.3 = (f32[864,128]{1,0:T(8,128)S(1)}, f32[720,128]{1,0:T(8,128)S(1)}, f32[432,128]{1,0:T(8,128)S(1)}) custom-call(s32[1]{0:T(128)S(6)} %copy.15.refs_0_, s32[256]{0:T(256)} %refs_1_.3, s32[256]{0:T(256)} %refs_2_.3, s32[256]{0:T(256)} %refs_3_.3, bf16[69,4,128]{2,1,0:T(4,128)(2,1)} %bitcast.7, bf16[256,128,128]{2,1,0:T(8,128)(2,1)} %refs_5_.3, ...), custom_call_target="tpu_custom_call" | custom-call | tf_op jit(solution)/shard_map/remap/pallas_call | solution.py:234
  12.4 0.0 copy-start
  12.4 1.8 %collective-permute-done.arrived_ref = bf16[864,128]{1,0:T(8,128)(2,1)S(1)} collective-permute-done((bf16[864,128]{1,0:T(8,128)(2,1)S(1)}, bf16[864,128]{1,0:T(8,128)(2,1)S(1)}, u32[]{:S(2)}, u32[]{:S(2)}) %collective-permute-start) | collective-permute-done | bytes 221216 | tf_op jit(solution)/shard_map/ppermute | solution.py:495
  14.3 3.1 %collective-permute-start.1 = (bf16[432,128]{1,0:T(8,128)(2,1)S(1)}, bf16[432,128]{1,0:T(8,128)(2,1)S(1)}, u32[]{:S(2)}, u32[]{:S(2)}) collective-permute-start(bf16[432,128]{1,0:T(8,128)(2,1)S(1)} %get-tuple-element.27.unread), channel_id=1, source_target_pairs={{0,8},{4,12},{8,0},{12,4},{1,9},{5,13},{9,1},{13,5},{2,10},{6,14},... | collective-permute-start | bytes 331784 | tf_op jit(solution)/shard_map/ppermute | solution.py:495
  17.4 0.0 copy-done.2
  17.4 1.9 %prepare.1 = (bf16[256,656]{1,0:T(8,128)(2,1)S(1)}, bf16[1024,216]{1,0:T(8,128)(2,1)S(1)}, bf16[1536,448]{1,0:T(8,128)(2,1)S(1)}) custom-call(s32[4,7]{1,0:T(4,128)S(1)} %bitcast.4, s32[4,7]{1,0:T(4,128)S(1)} %bitcast.5, bf16[9,69,256]{2,1,0:T(8,128)(2,1)S(1)} %copy-done.2, bf16[432,128]{1,0:T(8,128)(2,1)S(1)} %get-tuple-element.27.unread), custom_call_target="tpu_custom_call" | custom-call | tf_op jit(solution)/shard_map/prepare/pallas_call | solution.py:351
  19.3 1.6 %collective-permute-start.4 = (bf16[432,128]{1,0:T(8,128)(2,1)S(1)}, bf16[432,128]{1,0:T(8,128)(2,1)S(1)}, u32[]{:S(2)}, u32[]{:S(2)}) collective-permute-start(bf16[432,128]{1,0:T(8,128)(2,1)S(1)} %get-tuple-element.36), channel_id=1, source_target_pairs={{0,4},{4,0},{8,12},{12,8},{1,5},{5,1},{9,13},{13,9},{2,6},{6,2},{1... | collective-permute-start | bytes 331784 | tf_op jit(solution)/shard_map/ppermute | solution.py:495
  20.9 0.0 collective-permute-done.2.arrived_ref
  21.0 0.4 %collective-permute-start.3 = (bf16[360,128]{1,0:T(8,128)(2,1)S(1)}, bf16[360,128]{1,0:T(8,128)(2,1)S(1)}, u32[]{:S(2)}, u32[]{:S(2)}) collective-permute-start(bf16[360,128]{1,0:T(8,128)(2,1)S(1)} %get-tuple-element.32), channel_id=1, source_target_pairs={{0,8},{4,12},{8,0},{12,4},{1,9},{5,13},{9,1},{13,5},{2,10},{6,14},... | collective-permute-start | bytes 276488 | tf_op jit(solution)/shard_map/ppermute | solution.py:495
  21.4 0.0 collective-permute-done.1.refs_1_
  21.4 0.1 collective-permute-start.6
  21.5 4.4 %collective-permute-start.7 = (bf16[288,128]{1,0:T(8,128)(2,1)S(1)}, bf16[288,128]{1,0:T(8,128)(2,1)S(1)}, u32[]{:S(2)}, u32[]{:S(2)}) collective-permute-start(bf16[288,128]{1,0:T(8,128)(2,1)S(1)} %get-tuple-element.40.own_ref), channel_id=1, source_target_pairs={{0,15},{1,0},{2,1},{3,2},{4,3},{5,4},{6,5},{7,6},{8,7},{9,8},{10,9... | collective-permute-start | bytes 221192 | tf_op jit(solution)/shard_map/ppermute | solution.py:589
  25.9 0.0 collective-permute-done.4.arrived_ref
  26.0 1.0 %collective-permute-start.5 = (bf16[216,128]{1,0:T(8,128)(2,1)S(1)}, bf16[216,128]{1,0:T(8,128)(2,1)S(1)}, u32[]{:S(2)}, u32[]{:S(2)}) collective-permute-start(bf16[216,128]{1,0:T(8,128)(2,1)S(1)} %get-tuple-element.38), channel_id=1, source_target_pairs={{0,8},{4,12},{8,0},{12,4},{1,9},{5,13},{9,1},{13,5},{2,10},{6,14},... | collective-permute-start | bytes 165896 | tf_op jit(solution)/shard_map/ppermute | solution.py:495
  27.0 1.2 %collective-permute-done.6.near_ref = bf16[288,128]{1,0:T(8,128)(2,1)S(1)} collective-permute-done((bf16[288,128]{1,0:T(8,128)(2,1)S(1)}, bf16[288,128]{1,0:T(8,128)(2,1)S(1)}, u32[]{:S(2)}, u32[]{:S(2)}) %collective-permute-start.6) | collective-permute-done | bytes 73760 | tf_op jit(solution)/shard_map/ppermute | solution.py:589
  28.2 0.0 collective-permute-done.7.far_ref
  28.2 0.0 copy-start.3
  28.2 1.3 %rims.1.refs_6_ = bf16[256,448]{1,0:T(8,128)(2,1)S(1)} custom-call(bf16[288,128]{1,0:T(8,128)(2,1)S(1)} %collective-permute-done.6.near_ref, bf16[288,128]{1,0:T(8,128)(2,1)S(1)} %get-tuple-element.40.own_ref, bf16[288,128]{1,0:T(8,128)(2,1)S(1)} %collective-permute-done.7.far_ref, bf16[1024,216]{1,0:T(8,128)(2,1)S(1)} %get-tuple-element.41.weight_ref, ...), custom_call_target="tpu_custom_call" | custom-call | tf_op jit(solution)/shard_map/rims/pallas_call | solution.py:414
  29.5 0.0 collective-permute-done.3.refs_2_
  29.5 1.6 %collective-permute-done.5.refs_4_ = bf16[216,128]{1,0:T(8,128)(2,1)S(1)} collective-permute-done((bf16[216,128]{1,0:T(8,128)(2,1)S(1)}, bf16[216,128]{1,0:T(8,128)(2,1)S(1)}, u32[]{:S(2)}, u32[]{:S(2)}) %collective-permute-start.5) | collective-permute-done | bytes 55328 | tf_op jit(solution)/shard_map/ppermute | solution.py:495
  31.1 2.6 %convolve.1 = bf16[7,256,256]{2,1,0:T(8,128)(2,1)} custom-call(bf16[432,128]{1,0:T(8,128)(2,1)S(1)} %get-tuple-element.28.refs_0_, f32[360,128]{1,0:T(8,128)S(1)} %get-tuple-element.31.refs_1_, bf16[360,128]{1,0:T(8,128)(2,1)S(1)} %collective-permute-done.3.refs_2_, f32[216,128]{1,0:T(8,128)S(1)} %get-tuple-element.37.refs_3_, ...), custom_call_target="tpu_custom_call" | custom-call | tf_op jit(solution)/shard_map/convolve/pallas_call | solution.py:473
  (13 shorter events, 0.1 us)
Async XLA Ops:
  4.9 9.4 %collective-permute-start = (bf16[864,128]{1,0:T(8,128)(2,1)S(1)}, bf16[864,128]{1,0:T(8,128)(2,1)S(1)}, u32[]{:S(2)}, u32[]{:S(2)}) collective-permute-start(bf16[864,128]{1,0:T(8,128)(2,1)S(1)} %get-tuple-element.24.refs_7_), channel_id=1, source_target_pairs={{0,4},{4,0},{8,12},{12,8},{1,5},{5,1},{9,13},{13,9},{2,6},{6,2},{1... | collective-permute-start | bytes 663560 | tf_op jit(solution)/shard_map/ppermute | solution.py:495
  8.0 9.4 %copy-start.2 = (bf16[9,69,256]{2,1,0:T(8,128)(2,1)S(1)}, bf16[9,69,256]{2,1,0:T(8,128)(2,1)}, u32[]{:S(2)}) copy-start(bf16[9,69,256]{2,1,0:T(8,128)(2,1)} %taps_ref.1) | copy-start | bytes 953860
  8.0 9.4 %copy-start.4 = (s32[7,4]{0,1:T(4,128)S(1)}, s32[7,4]{0,1:T(4,128)}, u32[]{:S(2)}) copy-start(s32[7,4]{0,1:T(4,128)} %param.21) | copy-start | bytes 340
  8.0 9.4 %copy-start.5 = (s32[7,4]{0,1:T(4,128)S(1)}, s32[7,4]{0,1:T(4,128)}, u32[]{:S(2)}) copy-start(s32[7,4]{0,1:T(4,128)} %param.22) | copy-start | bytes 340
  8.0 12.9 %collective-permute-start.2 = (bf16[720,128]{1,0:T(8,128)(2,1)S(1)}, bf16[720,128]{1,0:T(8,128)(2,1)S(1)}, u32[]{:S(2)}, u32[]{:S(2)}) collective-permute-start(bf16[720,128]{1,0:T(8,128)(2,1)S(1)} %get-tuple-element.30), channel_id=1, source_target_pairs={{0,4},{4,0},{8,12},{12,8},{1,5},{5,1},{9,13},{13,9},{2,6},{6,2},{1... | collective-permute-start | bytes 552968 | tf_op jit(solution)/shard_map/ppermute | solution.py:495
  12.4 15.7 %copy-start = (bf16[512,1536]{1,0:T(8,128)(2,1)S(1)}, bf16[512,1536]{1,0:T(8,128)(2,1)}, u32[]{:S(2)}) copy-start(bf16[512,1536]{1,0:T(8,128)(2,1)} %constant.9.clone.edge_ref) | copy-start | bytes 4718596
  14.3 7.1 %collective-permute-start.1 = (bf16[432,128]{1,0:T(8,128)(2,1)S(1)}, bf16[432,128]{1,0:T(8,128)(2,1)S(1)}, u32[]{:S(2)}, u32[]{:S(2)}) collective-permute-start(bf16[432,128]{1,0:T(8,128)(2,1)S(1)} %get-tuple-element.27.unread), channel_id=1, source_target_pairs={{0,8},{4,12},{8,0},{12,4},{1,9},{5,13},{9,1},{13,5},{2,10},{6,14},... | collective-permute-start | bytes 331784 | tf_op jit(solution)/shard_map/ppermute | solution.py:495
  19.3 6.6 %collective-permute-start.4 = (bf16[432,128]{1,0:T(8,128)(2,1)S(1)}, bf16[432,128]{1,0:T(8,128)(2,1)S(1)}, u32[]{:S(2)}, u32[]{:S(2)}) collective-permute-start(bf16[432,128]{1,0:T(8,128)(2,1)S(1)} %get-tuple-element.36), channel_id=1, source_target_pairs={{0,4},{4,0},{8,12},{12,8},{1,5},{5,1},{9,13},{13,9},{2,6},{6,2},{1... | collective-permute-start | bytes 331784 | tf_op jit(solution)/shard_map/ppermute | solution.py:495
  21.0 8.6 %collective-permute-start.3 = (bf16[360,128]{1,0:T(8,128)(2,1)S(1)}, bf16[360,128]{1,0:T(8,128)(2,1)S(1)}, u32[]{:S(2)}, u32[]{:S(2)}) collective-permute-start(bf16[360,128]{1,0:T(8,128)(2,1)S(1)} %get-tuple-element.32), channel_id=1, source_target_pairs={{0,8},{4,12},{8,0},{12,4},{1,9},{5,13},{9,1},{13,5},{2,10},{6,14},... | collective-permute-start | bytes 276488 | tf_op jit(solution)/shard_map/ppermute | solution.py:495
  21.4 6.7 %collective-permute-start.6 = (bf16[288,128]{1,0:T(8,128)(2,1)S(1)}, bf16[288,128]{1,0:T(8,128)(2,1)S(1)}, u32[]{:S(2)}, u32[]{:S(2)}) collective-permute-start(bf16[288,128]{1,0:T(8,128)(2,1)S(1)} %get-tuple-element.40.own_ref), channel_id=1, source_target_pairs={{0,1},{1,2},{2,3},{3,4},{4,5},{5,6},{6,7},{7,8},{8,9},{9,10},{10,1... | collective-permute-start | bytes 221192 | tf_op jit(solution)/shard_map/ppermute | solution.py:589
  21.5 6.7 %collective-permute-start.7 = (bf16[288,128]{1,0:T(8,128)(2,1)S(1)}, bf16[288,128]{1,0:T(8,128)(2,1)S(1)}, u32[]{:S(2)}, u32[]{:S(2)}) collective-permute-start(bf16[288,128]{1,0:T(8,128)(2,1)S(1)} %get-tuple-element.40.own_ref), channel_id=1, source_target_pairs={{0,15},{1,0},{2,1},{3,2},{4,3},{5,4},{6,5},{7,6},{8,7},{9,8},{10,9... | collective-permute-start | bytes 221192 | tf_op jit(solution)/shard_map/ppermute | solution.py:589
  26.0 5.1 %collective-permute-start.5 = (bf16[216,128]{1,0:T(8,128)(2,1)S(1)}, bf16[216,128]{1,0:T(8,128)(2,1)S(1)}, u32[]{:S(2)}, u32[]{:S(2)}) collective-permute-start(bf16[216,128]{1,0:T(8,128)(2,1)S(1)} %get-tuple-element.38), channel_id=1, source_target_pairs={{0,8},{4,12},{8,0},{12,4},{1,9},{5,13},{9,1},{13,5},{2,10},{6,14},... | collective-permute-start | bytes 165896 | tf_op jit(solution)/shard_map/ppermute | solution.py:495
  28.2 2.9 %copy-start.1 = (bf16[9,256,256]{2,1,0:T(8,128)(2,1)S(1)}, bf16[9,256,256]{2,1,0:T(8,128)(2,1)}, u32[]{:S(2)}) copy-start(bf16[9,256,256]{2,1,0:T(8,128)(2,1)} %constant.10.clone.refs_7_) | copy-start | bytes 3538948
  28.2 2.9 %copy-start.3 = (bf16[64,256]{1,0:T(8,128)(2,1)S(1)}, bf16[64,256]{1,0:T(8,128)(2,1)}, u32[]{:S(2)}) copy-start(bf16[64,256]{1,0:T(8,128)(2,1)} %constant.11.clone.refs_8_) | copy-start | bytes 98308

commit v3 on v2

--- a/solution.py
+++ b/solution.py
@@ -217,8 +217,7 @@
                 axis=0,
             )
             for ref, (first, last) in zip(out_refs, pieces):
-                size = last - first
-                ref[size * index : size * (index + 1)] = rows[first:last].astype(kind)
+                ref[index] = rows[first:last].astype(kind)
 
     operands = [
         pltpu.with_memory_space_constraint(operand, pltpu.HBM)
@@ -238,7 +237,7 @@
         + [pl.BlockSpec(memory_space=pl.ANY)] * len(after),
         out_specs=[pl.BlockSpec(memory_space=pltpu.VMEM)] * len(pieces),
         out_shape=[
-            jax.ShapeDtypeStruct((count * (last - first), half), kind) for first, last in pieces
+            jax.ShapeDtypeStruct((count, last - first, half), kind) for first, last in pieces
         ],
         scratch_shapes=[
             pltpu.SMEM((slots,), jnp.int32),
@@ -258,12 +257,10 @@
 
 
 def add_halves(kept, arrived, after=()):
-    rows = kept.shape[0] // 2
-
     def kernel(kept_ref, arrived_ref, *refs):
         here_ref, there_ref = refs[len(after) :]
-        here_ref[...] = kept_ref[:rows] + arrived_ref[:rows].astype(F32)
-        there_ref[...] = (kept_ref[rows:] + arrived_ref[rows:].astype(F32)).astype(BF16)
+        here_ref[...] = kept_ref[0] + arrived_ref[0].astype(F32)
+        there_ref[...] = (kept_ref[1] + arrived_ref[1].astype(F32)).astype(BF16)
 
     vmem = pl.BlockSpec(memory_space=pltpu.VMEM)
     return pl.pallas_call(
@@ -271,8 +268,8 @@
         in_specs=[vmem] * 2 + [pl.BlockSpec(memory_space=pl.ANY)] * len(after),
         out_specs=[vmem] * 2,
         out_shape=[
-            jax.ShapeDtypeStruct((rows, kept.shape[1]), F32),
-            jax.ShapeDtypeStruct((rows, kept.shape[1]), BF16),
+            jax.ShapeDtypeStruct(kept.shape[1:], F32),
+            jax.ShapeDtypeStruct(kept.shape[1:], BF16),
         ],
         compiler_params=pltpu.CompilerParams(vmem_limit_bytes=VMEM_LIMIT),
         name="add_halves",
@@ -321,7 +318,8 @@
         for tap in range(taps):
             rows.append(jnp.concatenate([taps_ref[tap].astype(F32), empty], axis=0))
         tail = jnp.zeros((rest - taps * (padded - full), hidden), F32)
-        stacked = [row[:full] for row in rows] + [row[full:] for row in rows] + [tail]
+        lead = jnp.zeros((4 * SIDE, hidden), F32)
+        stacked = [lead] + [row[:full] for row in rows] + [row[full:] for row in rows] + [tail]
         weight_ref[...] = jnp.concatenate(stacked, axis=0).T.astype(BF16)
         for side in range(4):
             chosen = [rows[tap] for tap in rim_taps(side)]
@@ -353,7 +351,7 @@
         in_specs=[smem, smem, vmem, pl.BlockSpec(memory_space=pl.ANY)],
         out_specs=[vmem] * 3,
         out_shape=[
-            jax.ShapeDtypeStruct((hidden, taps * full + rest), BF16),
+            jax.ShapeDtypeStruct((hidden, 4 * SIDE + taps * full + rest), BF16),
             jax.ShapeDtypeStruct((4 * hidden, 3 * padded), BF16),
             jax.ShapeDtypeStruct((columns, slots), BF16),
         ],
@@ -407,13 +405,13 @@
                     preferred_element_type=F32,
                 ).astype(BF16)
             )
-        out_ref[...] = jnp.dot(
+        out_ref[:, :slots] = jnp.dot(
             jnp.concatenate(rims, axis=1), pick_ref[...], preferred_element_type=F32
         ).astype(BF16)
 
     return pl.pallas_call(
         kernel,
-        out_shape=jax.ShapeDtypeStruct((hidden, slots), BF16),
+        out_shape=jax.ShapeDtypeStruct((hidden, pairs * LANES), BF16),
         compiler_params=pltpu.CompilerParams(vmem_limit_bytes=VMEM_LIMIT),
         name="rims",
     )(*edges, rim_weight, pick, constant(edge_matrix(pairs)))
@@ -450,18 +448,20 @@
         for tap in range(TAPS):
             moved = jnp.dot(cells, shift_ref[tap], preferred_element_type=F32)
             moved = moved.reshape(blocks, padded, CELLS)
-            stack[:, full * tap : full * (tap + 1), :] = moved[:, :full].astype(BF16)
+            first = 4 * SIDE + full * tap
+            stack[:, first : first + full, :] = moved[:, :full].astype(BF16)
             rests.append(moved[:, full:])
         rests.append(jnp.zeros((blocks, rest - TAPS * (padded - full), CELLS), F32))
-        stack[:, full * TAPS :, :] = jnp.concatenate(rests, axis=1).astype(BF16)
+        stack[:, 4 * SIDE + full * TAPS :, :] = jnp.concatenate(rests, axis=1).astype(BF16)
+        lane = lax.broadcasted_iota(jnp.int32, (hidden, LANES), 1)
         for index, block in enumerate(order):
-            grad = jnp.dot(
-                weight_ref[...], stack[index], preferred_element_type=F32
-            ) + jnp.dot(
-                incoming_ref[:, 64 * block : 64 * (block + 1)],
-                place_ref[...],
-                preferred_element_type=F32,
-            )
+            stack[index, : 4 * SIDE, :] = place_ref[...]
+            pair = incoming_ref[:, LANES * (block // 2) : LANES * (block // 2 + 1)].astype(F32)
+            if block % 2:
+                pair = pltpu.roll(pair, 64, 1)
+            ahead = jnp.where(lane < 4 * SIDE, pair, weight_ref[:, :LANES].astype(F32))
+            mixed = jnp.concatenate([ahead.astype(BF16), weight_ref[:, LANES:]], axis=1)
+            grad = jnp.dot(mixed, stack[index], preferred_element_type=F32)
             result[block] = grad.astype(BF16)
             copies.append(
                 pltpu.make_async_copy(result.at[block], out_ref.at[block], sems.at[block])
@@ -475,7 +475,7 @@
         out_shape=jax.ShapeDtypeStruct((blocks, hidden, CELLS), BF16),
         out_specs=pl.BlockSpec(memory_space=pltpu.HBM),
         scratch_shapes=[
-            pltpu.VMEM((blocks, TAPS * full + rest, CELLS), BF16),
+            pltpu.VMEM((blocks, 4 * SIDE + TAPS * full + rest, CELLS), BF16),
             pltpu.VMEM((blocks, hidden, CELLS), BF16),
             pltpu.SemaphoreType.DMA((blocks,)),
         ],

time: 33.9 us -> 33.7 us (level)
  no operation moved by 1% of the time
where the time goes in v3:
time: 33.7 us; the launch traced here: 33.5 us
  Pallas kernels  14.3 us (42%)
  starting transfers between devices  13.8 us (41%)
  waiting for transfers between devices  4.61 us (14%)
  between operations  0.74 us (2%)
    ppermute x6, starting transfers between devices, swapped(): return lax.ppermute(value, 'tile', pairs)  9.35 us
    pallas_call x2, Pallas kernels, remap_runs(): pl.pallas_call(kernel, in_specs=[pl.BlockSpec(memory_space=pltpu.SMEM)] +...  8.52 us
    ppermute x2, starting transfers between devices, per_device(): lax.ppermute(edges, ('tile', 'chan'), pairs)  4.49 us
    ppermute x6, waiting for transfers between devices, swapped(): return lax.ppermute(value, 'tile', pairs)  3.4 us
    pallas_call x1, Pallas kernels, convolve(): pl.pallas_call(kernel, out_shape=jax.ShapeDtypeStruct((blocks, hidden, CE...  2.38 us
    pallas_call x1, Pallas kernels, prepare(): pl.pallas_call(kernel, in_specs=[smem, smem, vmem, pl.BlockSpec(memory_sp...  1.94 us
    pallas_call x1, Pallas kernels, incoming_rims(): pl.pallas_call(kernel, out_shape=jax.ShapeDtypeStruct((hidden, pairs * LA...  1.32 us
    ppermute x2, waiting for transfers between devices, per_device(): lax.ppermute(edges, ('tile', 'chan'), pairs)  1.21 us
  transfers between devices with their start and end apart: 8, of which 3 were waited for; matrix products, arithmetic and copies ran while one was open for 0% of the time, Pallas kernels for 23%

profile of v3, /device:TPU:0, one launch (start us, length us, event | category | flops | bytes accessed | tf_op | source)
XLA Modules:
  0.0 33.5 jit_solution(12887924160935503577)
XLA Ops:
  0.7 4.2 %remap.2 = (bf16[2,432,128]{2,1,0:T(8,128)(2,1)S(1)}, bf16[2,360,128]{2,1,0:T(8,128)(2,1)S(1)}, bf16[2,216,128]{2,1,0:T(8,128)(2,1)S(1)}) custom-call(s32[1]{0:T(128)S(6)} %copy.15.refs_0_, s32[256]{0:T(256)} %refs_1_.3, s32[256]{0:T(256)} %refs_2_.3, s32[256]{0:T(256)} %refs_3_.3, bf16[69,4,128]{2,1,0:T(4,128)(2,1)} %bitcast.6, ...), custom_call_target="tpu_custom_call" | custom-call | tf_op jit(solution)/shard_map/remap/pallas_call | solution.py:233
  4.9 3.1 %collective-permute-start = (bf16[2,432,128]{2,1,0:T(8,128)(2,1)S(1)}, bf16[2,432,128]{2,1,0:T(8,128)(2,1)S(1)}, u32[]{:S(2)}, u32[]{:S(2)}) collective-permute-start(bf16[2,432,128]{2,1,0:T(8,128)(2,1)S(1)} %get-tuple-element.24.refs_7_), channel_id=1, source_target_pairs={{0,4},{4,0},{8,12},{12,8},{1,5},{5,1},{9,13},{13,9},{2,6},{6,2},{1... | collective-permute-start | bytes 663560 | tf_op jit(solution)/shard_map/ppermute | solution.py:495
  8.0 0.1 collective-permute-start.2
  8.1 4.3 %remap.3 = (f32[2,432,128]{2,1,0:T(8,128)S(1)}, f32[2,360,128]{2,1,0:T(8,128)S(1)}, f32[2,216,128]{2,1,0:T(8,128)S(1)}) custom-call(s32[1]{0:T(128)S(6)} %copy.15.refs_0_, s32[256]{0:T(256)} %refs_1_.3, s32[256]{0:T(256)} %refs_2_.3, s32[256]{0:T(256)} %refs_3_.3, bf16[69,4,128]{2,1,0:T(4,128)(2,1)} %bitcast.7, bf16[256,128,128]{2,1,0:T(8,128)(2,1)} %refs_5_.3, ...), custom_call_target="tpu_custom_call" | custom-call | tf_op jit(solution)/shard_map/remap/pallas_call | solution.py:233
  12.4 0.0 copy-start
  12.4 1.8 %collective-permute-done.arrived_ref = bf16[2,432,128]{2,1,0:T(8,128)(2,1)S(1)} collective-permute-done((bf16[2,432,128]{2,1,0:T(8,128)(2,1)S(1)}, bf16[2,432,128]{2,1,0:T(8,128)(2,1)S(1)}, u32[]{:S(2)}, u32[]{:S(2)}) %collective-permute-start) | collective-permute-done | bytes 221216 | tf_op jit(solution)/shard_map/ppermute | solution.py:495
  14.3 3.2 %collective-permute-start.1 = (bf16[432,128]{1,0:T(8,128)(2,1)S(1)}, bf16[432,128]{1,0:T(8,128)(2,1)S(1)}, u32[]{:S(2)}, u32[]{:S(2)}) collective-permute-start(bf16[432,128]{1,0:T(8,128)(2,1)S(1)} %get-tuple-element.27.unread), channel_id=1, source_target_pairs={{0,8},{4,12},{8,0},{12,4},{1,9},{5,13},{9,1},{13,5},{2,10},{6,14},... | collective-permute-start | bytes 331784 | tf_op jit(solution)/shard_map/ppermute | solution.py:495
  17.4 0.0 copy-done.2
  17.4 1.9 %prepare.1 = (bf16[256,720]{1,0:T(8,128)(2,1)S(1)}, bf16[1024,216]{1,0:T(8,128)(2,1)S(1)}, bf16[1536,448]{1,0:T(8,128)(2,1)S(1)}) custom-call(s32[4,7]{1,0:T(4,128)S(1)} %bitcast.4, s32[4,7]{1,0:T(4,128)S(1)} %bitcast.5, bf16[9,69,256]{2,1,0:T(8,128)(2,1)S(1)} %copy-done.2, bf16[432,128]{1,0:T(8,128)(2,1)S(1)} %get-tuple-element.27.unread), custom_call_target="tpu_custom_call" | custom-call | tf_op jit(solution)/shard_map/prepare/pallas_call | solution.py:349
  19.4 1.6 %collective-permute-start.4 = (bf16[2,216,128]{2,1,0:T(8,128)(2,1)S(1)}, bf16[2,216,128]{2,1,0:T(8,128)(2,1)S(1)}, u32[]{:S(2)}, u32[]{:S(2)}) collective-permute-start(bf16[2,216,128]{2,1,0:T(8,128)(2,1)S(1)} %get-tuple-element.36), channel_id=1, source_target_pairs={{0,4},{4,0},{8,12},{12,8},{1,5},{5,1},{9,13},{13,9},{2,6},{6,2},{1... | collective-permute-start | bytes 331784 | tf_op jit(solution)/shard_map/ppermute | solution.py:495
  21.0 0.0 collective-permute-done.2.arrived_ref
  21.0 0.4 %collective-permute-start.3 = (bf16[360,128]{1,0:T(8,128)(2,1)S(1)}, bf16[360,128]{1,0:T(8,128)(2,1)S(1)}, u32[]{:S(2)}, u32[]{:S(2)}) collective-permute-start(bf16[360,128]{1,0:T(8,128)(2,1)S(1)} %get-tuple-element.32), channel_id=1, source_target_pairs={{0,8},{4,12},{8,0},{12,4},{1,9},{5,13},{9,1},{13,5},{2,10},{6,14},... | collective-permute-start | bytes 276488 | tf_op jit(solution)/shard_map/ppermute | solution.py:495
  21.4 0.0 collective-permute-done.1.refs_1_
  21.5 0.1 collective-permute-start.6
  21.5 4.4 %collective-permute-start.7 = (bf16[288,128]{1,0:T(8,128)(2,1)S(1)}, bf16[288,128]{1,0:T(8,128)(2,1)S(1)}, u32[]{:S(2)}, u32[]{:S(2)}) collective-permute-start(bf16[288,128]{1,0:T(8,128)(2,1)S(1)} %get-tuple-element.40.own_ref), channel_id=1, source_target_pairs={{0,15},{1,0},{2,1},{3,2},{4,3},{5,4},{6,5},{7,6},{8,7},{9,8},{10,9... | collective-permute-start | bytes 221192 | tf_op jit(solution)/shard_map/ppermute | solution.py:589
  26.0 0.0 collective-permute-done.4.arrived_ref
  26.0 1.0 %collective-permute-start.5 = (bf16[216,128]{1,0:T(8,128)(2,1)S(1)}, bf16[216,128]{1,0:T(8,128)(2,1)S(1)}, u32[]{:S(2)}, u32[]{:S(2)}) collective-permute-start(bf16[216,128]{1,0:T(8,128)(2,1)S(1)} %get-tuple-element.38), channel_id=1, source_target_pairs={{0,8},{4,12},{8,0},{12,4},{1,9},{5,13},{9,1},{13,5},{2,10},{6,14},... | collective-permute-start | bytes 165896 | tf_op jit(solution)/shard_map/ppermute | solution.py:495
  27.0 1.2 %collective-permute-done.6.near_ref = bf16[288,128]{1,0:T(8,128)(2,1)S(1)} collective-permute-done((bf16[288,128]{1,0:T(8,128)(2,1)S(1)}, bf16[288,128]{1,0:T(8,128)(2,1)S(1)}, u32[]{:S(2)}, u32[]{:S(2)}) %collective-permute-start.6) | collective-permute-done | bytes 73760 | tf_op jit(solution)/shard_map/ppermute | solution.py:589
  28.2 0.0 collective-permute-done.7.far_ref
  28.2 0.0 copy-start.3
  28.2 1.3 %rims.1.refs_6_ = bf16[256,512]{1,0:T(8,128)(2,1)S(1)} custom-call(bf16[288,128]{1,0:T(8,128)(2,1)S(1)} %collective-permute-done.6.near_ref, bf16[288,128]{1,0:T(8,128)(2,1)S(1)} %get-tuple-element.40.own_ref, bf16[288,128]{1,0:T(8,128)(2,1)S(1)} %collective-permute-done.7.far_ref, bf16[1024,216]{1,0:T(8,128)(2,1)S(1)} %get-tuple-element.41.weight_ref, ...), custom_call_target="tpu_custom_call" | custom-call | tf_op jit(solution)/shard_map/rims/pallas_call | solution.py:412
  29.5 0.0 collective-permute-done.3.refs_2_
  29.5 1.6 %collective-permute-done.5.refs_4_ = bf16[216,128]{1,0:T(8,128)(2,1)S(1)} collective-permute-done((bf16[216,128]{1,0:T(8,128)(2,1)S(1)}, bf16[216,128]{1,0:T(8,128)(2,1)S(1)}, u32[]{:S(2)}, u32[]{:S(2)}) %collective-permute-start.5) | collective-permute-done | bytes 55328 | tf_op jit(solution)/shard_map/ppermute | solution.py:495
  31.1 2.4 %convolve.1 = bf16[7,256,256]{2,1,0:T(8,128)(2,1)} custom-call(bf16[432,128]{1,0:T(8,128)(2,1)S(1)} %get-tuple-element.28.refs_0_, f32[360,128]{1,0:T(8,128)S(1)} %get-tuple-element.31.refs_1_, bf16[360,128]{1,0:T(8,128)(2,1)S(1)} %collective-permute-done.3.refs_2_, f32[216,128]{1,0:T(8,128)S(1)} %get-tuple-element.37.refs_3_, ...), custom_call_target="tpu_custom_call" | custom-call | tf_op jit(solution)/shard_map/convolve/pallas_call | solution.py:473
  (13 shorter events, 0.1 us)
Async XLA Ops:
  4.9 9.4 %collective-permute-start = (bf16[2,432,128]{2,1,0:T(8,128)(2,1)S(1)}, bf16[2,432,128]{2,1,0:T(8,128)(2,1)S(1)}, u32[]{:S(2)}, u32[]{:S(2)}) collective-permute-start(bf16[2,432,128]{2,1,0:T(8,128)(2,1)S(1)} %get-tuple-element.24.refs_7_), channel_id=1, source_target_pairs={{0,4},{4,0},{8,12},{12,8},{1,5},{5,1},{9,13},{13,9},{2,6},{6,2},{1... | collective-permute-start | bytes 663560 | tf_op jit(solution)/shard_map/ppermute | solution.py:495
  8.0 9.5 %copy-start.2 = (bf16[9,69,256]{2,1,0:T(8,128)(2,1)S(1)}, bf16[9,69,256]{2,1,0:T(8,128)(2,1)}, u32[]{:S(2)}) copy-start(bf16[9,69,256]{2,1,0:T(8,128)(2,1)} %taps_ref.1) | copy-start | bytes 953860
  8.0 9.5 %copy-start.4 = (s32[7,4]{0,1:T(4,128)S(1)}, s32[7,4]{0,1:T(4,128)}, u32[]{:S(2)}) copy-start(s32[7,4]{0,1:T(4,128)} %param.21) | copy-start | bytes 340
  8.0 9.5 %copy-start.5 = (s32[7,4]{0,1:T(4,128)S(1)}, s32[7,4]{0,1:T(4,128)}, u32[]{:S(2)}) copy-start(s32[7,4]{0,1:T(4,128)} %param.22) | copy-start | bytes 340
  8.0 13.0 %collective-permute-start.2 = (bf16[2,360,128]{2,1,0:T(8,128)(2,1)S(1)}, bf16[2,360,128]{2,1,0:T(8,128)(2,1)S(1)}, u32[]{:S(2)}, u32[]{:S(2)}) collective-permute-start(bf16[2,360,128]{2,1,0:T(8,128)(2,1)S(1)} %get-tuple-element.30), channel_id=1, source_target_pairs={{0,4},{4,0},{8,12},{12,8},{1,5},{5,1},{9,13},{13,9},{2,6},{6,2},{1... | collective-permute-start | bytes 552968 | tf_op jit(solution)/shard_map/ppermute | solution.py:495
  12.4 15.8 %copy-start = (bf16[512,1536]{1,0:T(8,128)(2,1)S(1)}, bf16[512,1536]{1,0:T(8,128)(2,1)}, u32[]{:S(2)}) copy-start(bf16[512,1536]{1,0:T(8,128)(2,1)} %constant.9.clone.edge_ref) | copy-start | bytes 4718596
  14.3 7.2 %collective-permute-start.1 = (bf16[432,128]{1,0:T(8,128)(2,1)S(1)}, bf16[432,128]{1,0:T(8,128)(2,1)S(1)}, u32[]{:S(2)}, u32[]{:S(2)}) collective-permute-start(bf16[432,128]{1,0:T(8,128)(2,1)S(1)} %get-tuple-element.27.unread), channel_id=1, source_target_pairs={{0,8},{4,12},{8,0},{12,4},{1,9},{5,13},{9,1},{13,5},{2,10},{6,14},... | collective-permute-start | bytes 331784 | tf_op jit(solution)/shard_map/ppermute | solution.py:495
  19.4 6.6 %collective-permute-start.4 = (bf16[2,216,128]{2,1,0:T(8,128)(2,1)S(1)}, bf16[2,216,128]{2,1,0:T(8,128)(2,1)S(1)}, u32[]{:S(2)}, u32[]{:S(2)}) collective-permute-start(bf16[2,216,128]{2,1,0:T(8,128)(2,1)S(1)} %get-tuple-element.36), channel_id=1, source_target_pairs={{0,4},{4,0},{8,12},{12,8},{1,5},{5,1},{9,13},{13,9},{2,6},{6,2},{1... | collective-permute-start | bytes 331784 | tf_op jit(solution)/shard_map/ppermute | solution.py:495
  21.0 8.5 %collective-permute-start.3 = (bf16[360,128]{1,0:T(8,128)(2,1)S(1)}, bf16[360,128]{1,0:T(8,128)(2,1)S(1)}, u32[]{:S(2)}, u32[]{:S(2)}) collective-permute-start(bf16[360,128]{1,0:T(8,128)(2,1)S(1)} %get-tuple-element.32), channel_id=1, source_target_pairs={{0,8},{4,12},{8,0},{12,4},{1,9},{5,13},{9,1},{13,5},{2,10},{6,14},... | collective-permute-start | bytes 276488 | tf_op jit(solution)/shard_map/ppermute | solution.py:495
  21.5 6.7 %collective-permute-start.6 = (bf16[288,128]{1,0:T(8,128)(2,1)S(1)}, bf16[288,128]{1,0:T(8,128)(2,1)S(1)}, u32[]{:S(2)}, u32[]{:S(2)}) collective-permute-start(bf16[288,128]{1,0:T(8,128)(2,1)S(1)} %get-tuple-element.40.own_ref), channel_id=1, source_target_pairs={{0,1},{1,2},{2,3},{3,4},{4,5},{5,6},{6,7},{7,8},{8,9},{9,10},{10,1... | collective-permute-start | bytes 221192 | tf_op jit(solution)/shard_map/ppermute | solution.py:589
  21.5 6.6 %collective-permute-start.7 = (bf16[288,128]{1,0:T(8,128)(2,1)S(1)}, bf16[288,128]{1,0:T(8,128)(2,1)S(1)}, u32[]{:S(2)}, u32[]{:S(2)}) collective-permute-start(bf16[288,128]{1,0:T(8,128)(2,1)S(1)} %get-tuple-element.40.own_ref), channel_id=1, source_target_pairs={{0,15},{1,0},{2,1},{3,2},{4,3},{5,4},{6,5},{7,6},{8,7},{9,8},{10,9... | collective-permute-start | bytes 221192 | tf_op jit(solution)/shard_map/ppermute | solution.py:589
  26.0 5.1 %collective-permute-start.5 = (bf16[216,128]{1,0:T(8,128)(2,1)S(1)}, bf16[216,128]{1,0:T(8,128)(2,1)S(1)}, u32[]{:S(2)}, u32[]{:S(2)}) collective-permute-start(bf16[216,128]{1,0:T(8,128)(2,1)S(1)} %get-tuple-element.38), channel_id=1, source_target_pairs={{0,8},{4,12},{8,0},{12,4},{1,9},{5,13},{9,1},{13,5},{2,10},{6,14},... | collective-permute-start | bytes 165896 | tf_op jit(solution)/shard_map/ppermute | solution.py:495
  28.2 2.9 %copy-start.1 = (bf16[9,256,256]{2,1,0:T(8,128)(2,1)S(1)}, bf16[9,256,256]{2,1,0:T(8,128)(2,1)}, u32[]{:S(2)}) copy-start(bf16[9,256,256]{2,1,0:T(8,128)(2,1)} %constant.10.clone.refs_7_) | copy-start | bytes 3538948
  28.2 2.9 %copy-start.3 = (bf16[64,256]{1,0:T(8,128)(2,1)S(1)}, bf16[64,256]{1,0:T(8,128)(2,1)}, u32[]{:S(2)}) copy-start(bf16[64,256]{1,0:T(8,128)(2,1)} %constant.11.clone.refs_8_) | copy-start | bytes 98308
